TPU v7x, 32 devices: a whole 2x2x4 slice. The times are simulated.
32 devices in a mesh: grp: 4 (over x, core), ctx: 2 (over y), wsh: 4 (over z).
Axes of the slice: x: 2, y: 2, z: 4, core: 2. Of those that a mesh axis runs over, the one named last changes fastest.
Arguments:
- tokens: bfloat16 [16, 256, 1024], P(('grp', 'wsh'), 'ctx'), may hold values from -6 to 6
- cotangent: bfloat16 [16, 256, 1024], P(('grp', 'wsh'), 'ctx'), may hold values from -6 to 6
- norm_gain: bfloat16 [1024], P(('grp', 'ctx', 'wsh')), may hold values from 0.5 to 1.5
- project_weight: bfloat16 [1024, 3072], P(('grp', 'ctx', 'wsh')), may hold values from -0.1875 to 0.1875
- output_weight: bfloat16 [1024, 1024], P(('grp', 'ctx', 'wsh')), may hold values from -1 to 1
- centroids: bfloat16 [2, 1024], P(None, ('grp', 'ctx', 'wsh')), may hold values from -0.125 to 0.125
- expert_up: bfloat16 [2, 2, 1024, 4096], P('ctx', None, 'grp', 'wsh'), may hold values from -0.1875 to 0.1875
- expert_down: bfloat16 [2, 2, 4096, 1024], P('ctx', None, 'wsh', 'grp'), may hold values from -0.09375 to 0.09375
- sequence_lengths: int32 [16, 3], P(('grp', 'wsh')), may hold values from 1 to 128, 256 in all within a row
- block_order: int32 [16, 2], P(('grp', 'wsh')), may hold values from 0 to 1, each once within a row
- routes: int32 [16, 256, 1], P(('grp', 'wsh'), 'ctx'), may hold values from 0 to 1; in each aligned block of 128 rows (0 to 127, 128 to 255, ..., all dimensions but the last counted through in order) at most 80 rows name the same one
Outputs:
- output: bfloat16 [16, 256, 1024], P(('grp', 'wsh'), 'ctx')
- tokens_grad: float32 [16, 256, 1024], P(('grp', 'wsh'), 'ctx')
- norm_gain_grad: float32 [1024], P(('grp', 'ctx', 'wsh'))
- project_weight_grad: float32 [1024, 3072], P(('grp', 'ctx', 'wsh'))
- output_weight_grad: float32 [1024, 1024], P(('grp', 'ctx', 'wsh'))
- centroids_grad: float32 [2, 1024], P(None, ('grp', 'ctx', 'wsh'))
- expert_up_grad: float32 [2, 2, 1024, 4096], P('ctx', None, 'grp', 'wsh')
- expert_down_grad: float32 [2, 2, 4096, 1024], P('ctx', None, 'wsh', 'grp')
Inputs may be any that keep to these rules, and one draw needn't show every extreme that they name: `routes`: within the rows of one device no expert is named by more than 80 rows, and in some device's rows one expert is named by exactly 80. `sequence_lengths`: each group's lengths sum to 256; each group's longest sequence has exactly 128 tokens. `block_order`: each group's row is a permutation of the 2 block numbers.
All inputs are finite; a program needn't handle non-finite values.
Results may differ from a plain program's by a relative error of at most 0.02.
Values may be sent and summed in bfloat16 or wider, within the bound.
A program may use at most 192 MiB of HBM per device.

v0:
```python
import math

import jax
import jax.numpy as jnp
from jax import lax
from jax.sharding import PartitionSpec as P

HEADS = 16
HDIM = 64
BLK = 128


precise = lax.Precision.HIGHEST


def place_rows(order_row, lengths_row, total_rows):
    row_index = jnp.arange(total_rows, dtype=jnp.int32)
    picked = (row_index // BLK)[:, None] == jnp.arange(order_row.shape[0], dtype=jnp.int32)[None, :]
    blocks = jnp.sum(jnp.where(picked, order_row[None, :], 0), axis=1)
    token_place = blocks * BLK + row_index % BLK
    bounds = jnp.cumsum(lengths_row)
    sequence = jnp.sum((token_place[:, None] >= bounds[None, :]).astype(jnp.int32), axis=1)
    return (token_place, sequence)


def normalize(values):
    average = jnp.mean(values, axis=-1, keepdims=True)
    centred = values - average
    inverse = lax.rsqrt(jnp.mean(centred * centred, axis=-1, keepdims=True) + 1e-05)
    return (centred * inverse, inverse)


def head_slice(matrix, section, offset, heads_per):
    width_part = heads_per * HDIM
    first_col = offset + section * width_part
    return matrix[:, first_col : first_col + width_part].reshape(matrix.shape[0], heads_per, HDIM)


def spread_rows(local_rows):
    return lax.all_gather(local_rows, "wsh", axis=0, tiled=True)


def collect_rows(partial_term):
    return lax.psum_scatter(
        partial_term.astype(jnp.bfloat16), "wsh", scatter_dimension=0, tiled=True
    ).astype(jnp.float32)


def trade_rows(slots_rows, peer_count, capacity):
    shaped = slots_rows.reshape(peer_count, capacity, slots_rows.shape[-1])
    moved = lax.all_to_all(shaped, "ctx", split_axis=0, concat_axis=0, tiled=True)
    return moved.reshape(peer_count * capacity, slots_rows.shape[-1])


def gelu_pullback(hidden, incoming):
    value_out, pullback = jax.vjp(jax.nn.gelu, hidden)
    return pullback(incoming)[0]


def shards(
    tokens,
    cotangent,
    norm_gain,
    project_weight,
    output_weight,
    centroids,
    expert_up,
    expert_down,
    sequence_lengths,
    block_order,
    routes,
):
    local_rows = tokens.shape[1]
    model_width = tokens.shape[2]
    peer_count = lax.axis_size("ctx")
    position = lax.axis_index("ctx")
    total_rows = local_rows * peer_count
    capacity = max(2, (5 * local_rows + 4 * peer_count - 1) // (4 * peer_count))
    slot_count = peer_count * capacity
    score_scale = 1.0 / math.sqrt(HDIM)
    heads_per = 4
    sections = HEADS // heads_per
    inputs_f = tokens[0].astype(jnp.float32)
    upstream = cotangent[0].astype(jnp.float32)
    project_full, output_full, gain_full, centroid_full = (
        lax.all_gather(project_weight, ("grp", "ctx", "wsh"), axis=0, tiled=True),
        lax.all_gather(output_weight, ("grp", "ctx", "wsh"), axis=0, tiled=True),
        lax.all_gather(norm_gain, ("grp", "ctx", "wsh"), axis=0, tiled=True),
        lax.all_gather(centroids, ("grp", "ctx", "wsh"), axis=1, tiled=True),
    )
    up_full, down_full = (
        lax.all_gather(expert_up, "grp", axis=2, tiled=True),
        lax.all_gather(expert_down, "grp", axis=3, tiled=True),
    )
    place_all, sequence_all = place_rows(block_order[0], sequence_lengths[0], total_rows)
    place_own = lax.dynamic_slice_in_dim(place_all, position * local_rows, local_rows)
    sequence_own = lax.dynamic_slice_in_dim(sequence_all, position * local_rows, local_rows)
    allowed = (sequence_own[:, None] == sequence_all[None, :]) & (
        place_all[None, :] <= place_own[:, None]
    )
    normed, inverse = normalize(inputs_f)
    gain_values = gain_full.astype(jnp.float32)
    normed_low = (normed * gain_values).astype(jnp.bfloat16)
    projected = jnp.dot(normed_low, project_full, preferred_element_type=jnp.float32)
    queries = projected[:, :model_width].astype(jnp.bfloat16)
    keyvalue = projected[:, model_width:].astype(jnp.bfloat16)
    keyvalue_all = lax.all_gather(keyvalue, "ctx", axis=0, tiled=True)
    mixed_parts = []
    logsum_parts = []
    for section in range(sections):
        head_query = head_slice(queries, section, 0, heads_per)
        head_key = head_slice(keyvalue_all, section, 0, heads_per)
        head_value = head_slice(keyvalue_all, section, model_width, heads_per)
        scores = (
            jnp.einsum("tgd,sgd->gts", head_query, head_key, preferred_element_type=jnp.float32)
            * score_scale
        )
        scores = jnp.where(allowed[None], scores, -1000000000.0)
        largest = jnp.max(scores, axis=-1, keepdims=True)
        exponent = jnp.exp(scores - largest)
        totals = jnp.sum(exponent, axis=-1, keepdims=True)
        weights = (exponent / totals).astype(jnp.bfloat16)
        mixed_part = jnp.einsum(
            "gts,sgd->tgd", weights, head_value, preferred_element_type=jnp.float32
        )
        mixed_parts.append(mixed_part.reshape(local_rows, heads_per * HDIM))
        logsum_parts.append((largest + jnp.log(totals))[:, :, 0])
    mixed_all = jnp.concatenate(mixed_parts, axis=1).astype(jnp.bfloat16)
    logsum = jnp.concatenate(logsum_parts, axis=0)
    after_attention = inputs_f + jnp.dot(mixed_all, output_full, preferred_element_type=jnp.float32)
    route_ids = routes[0, :, 0]
    member = route_ids[:, None] == jnp.arange(peer_count, dtype=jnp.int32)[None, :]
    member_f = member.astype(jnp.float32)
    picked_centroid = jnp.dot(member_f, centroid_full.astype(jnp.float32), precision=precise)
    gate_value = jax.nn.sigmoid(jnp.sum(after_attention * picked_centroid, axis=-1))
    member_int = member.astype(jnp.int32)
    ranking = jnp.sum((jnp.cumsum(member_int, axis=0) - 1) * member_int, axis=1)
    slot_index = route_ids * capacity + ranking
    dispatch = (slot_index[None, :] == jnp.arange(slot_count, dtype=jnp.int32)[:, None]).astype(
        jnp.bfloat16
    )
    sent_rows = jnp.dot(
        dispatch, after_attention.astype(jnp.bfloat16), preferred_element_type=jnp.float32
    ).astype(jnp.bfloat16)
    arrived = trade_rows(sent_rows, peer_count, capacity)
    up_first = up_full[0, 0]
    up_second = up_full[0, 1]
    down_first = down_full[0, 0]
    down_second = down_full[0, 1]
    gathered_one = spread_rows(arrived)
    hidden_one = jnp.dot(gathered_one, up_first, preferred_element_type=jnp.float32)
    active_one = jax.nn.gelu(hidden_one).astype(jnp.bfloat16)
    branch_one = collect_rows(jnp.dot(active_one, down_first, preferred_element_type=jnp.float32))
    middle = (arrived.astype(jnp.float32) + branch_one).astype(jnp.bfloat16)
    gathered_two = spread_rows(middle)
    hidden_two = jnp.dot(gathered_two, up_second, preferred_element_type=jnp.float32)
    active_two = jax.nn.gelu(hidden_two).astype(jnp.bfloat16)
    branch_two = collect_rows(jnp.dot(active_two, down_second, preferred_element_type=jnp.float32))
    expert_out = (branch_one + branch_two).astype(jnp.bfloat16)
    returned = trade_rows(expert_out, peer_count, capacity)
    returned_tok = jnp.einsum("st,sd->td", dispatch, returned, preferred_element_type=jnp.float32)
    output = after_attention + gate_value[:, None] * returned_tok
    gate_grad = jnp.sum(upstream * returned_tok, axis=-1)
    score_grad = gate_grad * gate_value * (1.0 - gate_value)
    centroid_term = jnp.dot(member_f.T, score_grad[:, None] * after_attention, precision=precise)
    branch_grad = (gate_value[:, None] * upstream).astype(jnp.bfloat16)
    branch_sent = jnp.dot(dispatch, branch_grad, preferred_element_type=jnp.float32).astype(
        jnp.bfloat16
    )
    branch_arrived = trade_rows(branch_sent, peer_count, capacity)
    grad_two = spread_rows(branch_arrived)
    hidden_two_grad = gelu_pullback(
        hidden_two, jnp.dot(grad_two, down_second.T, preferred_element_type=jnp.float32)
    ).astype(jnp.bfloat16)
    down_second_grad = jnp.dot(active_two.T, grad_two, preferred_element_type=jnp.float32)
    up_second_grad = jnp.dot(gathered_two.T, hidden_two_grad, preferred_element_type=jnp.float32)
    middle_grad = collect_rows(
        jnp.dot(hidden_two_grad, up_second.T, preferred_element_type=jnp.float32)
    )
    first_branch_grad = (branch_arrived.astype(jnp.float32) + middle_grad).astype(jnp.bfloat16)
    grad_one = spread_rows(first_branch_grad)
    hidden_one_grad = gelu_pullback(
        hidden_one, jnp.dot(grad_one, down_first.T, preferred_element_type=jnp.float32)
    ).astype(jnp.bfloat16)
    down_first_grad = jnp.dot(active_one.T, grad_one, preferred_element_type=jnp.float32)
    up_first_grad = jnp.dot(gathered_one.T, hidden_one_grad, preferred_element_type=jnp.float32)
    arrived_grad = (
        collect_rows(jnp.dot(hidden_one_grad, up_first.T, preferred_element_type=jnp.float32))
        + middle_grad
    ).astype(jnp.bfloat16)
    home_grad = trade_rows(arrived_grad, peer_count, capacity)
    home_grad_tok = jnp.einsum("st,sd->td", dispatch, home_grad, preferred_element_type=jnp.float32)
    up_terms = jnp.stack([up_first_grad, up_second_grad])[None]
    down_terms = jnp.stack([down_first_grad, down_second_grad])[None]
    up_grad_out, down_grad_out = (
        lax.psum_scatter(
            up_terms.astype(jnp.bfloat16), "grp", scatter_dimension=2, tiled=True
        ).astype(jnp.float32),
        lax.psum_scatter(
            down_terms.astype(jnp.bfloat16), "grp", scatter_dimension=3, tiled=True
        ).astype(jnp.float32),
    )
    residual_grad = upstream + score_grad[:, None] * picked_centroid + home_grad_tok
    residual_low = residual_grad.astype(jnp.bfloat16)
    output_term = jnp.dot(mixed_all.T, residual_low, preferred_element_type=jnp.float32)
    mixed_grad = jnp.dot(residual_low, output_full.T, preferred_element_type=jnp.float32).astype(
        jnp.bfloat16
    )
    query_grads = []
    key_grads = []
    value_grads = []
    delta_parts = []
    for section in range(sections):
        head_query = head_slice(queries, section, 0, heads_per)
        head_key = head_slice(keyvalue_all, section, 0, heads_per)
        head_value = head_slice(keyvalue_all, section, model_width, heads_per)
        head_grad = head_slice(mixed_grad, section, 0, heads_per)
        scores = (
            jnp.einsum("tgd,sgd->gts", head_query, head_key, preferred_element_type=jnp.float32)
            * score_scale
        )
        scores = jnp.where(allowed[None], scores, -1000000000.0)
        probs = jnp.exp(
            scores - logsum[section * heads_per : (section + 1) * heads_per][:, :, None]
        )
        probs_grad = jnp.einsum(
            "tgd,sgd->gts", head_grad, head_value, preferred_element_type=jnp.float32
        )
        row_delta = jnp.sum(probs_grad * probs, axis=-1)
        scores_grad = (probs * (probs_grad - row_delta[:, :, None])).astype(jnp.bfloat16)
        query_part = (
            jnp.einsum("gts,sgd->tgd", scores_grad, head_key, preferred_element_type=jnp.float32)
            * score_scale
        )
        query_grads.append(query_part.reshape(local_rows, heads_per * HDIM))
        delta_parts.append(row_delta)
        key_part = (
            jnp.einsum("gts,tgd->sgd", scores_grad, head_query, preferred_element_type=jnp.float32)
            * score_scale
        )
        value_part = jnp.einsum(
            "gts,tgd->sgd",
            probs.astype(jnp.bfloat16),
            head_grad,
            preferred_element_type=jnp.float32,
        )
        key_grads.append(key_part.reshape(total_rows, heads_per * HDIM))
        value_grads.append(value_part.reshape(total_rows, heads_per * HDIM))
    query_grad = jnp.concatenate(query_grads, axis=1).astype(jnp.bfloat16)
    keyvalue_terms = jnp.concatenate(key_grads + value_grads, axis=1)
    keyvalue_grad = lax.psum_scatter(
        keyvalue_terms.astype(jnp.bfloat16), "ctx", scatter_dimension=0, tiled=True
    )
    projected_grad = jnp.concatenate([query_grad, keyvalue_grad], axis=1)
    project_term = jnp.dot(normed_low.T, projected_grad, preferred_element_type=jnp.float32)
    normed_grad = jnp.dot(projected_grad, project_full.T, preferred_element_type=jnp.float32)
    gain_term = jnp.sum(normed_grad * normed, axis=0)
    scaled_grad = normed_grad * gain_values
    input_grad = residual_grad + inverse * (
        scaled_grad
        - jnp.mean(scaled_grad, axis=-1, keepdims=True)
        - normed * jnp.mean(scaled_grad * normed, axis=-1, keepdims=True)
    )
    project_grad, output_grad, gain_grad, centroid_grad = (
        lax.psum_scatter(project_term, ("grp", "ctx", "wsh"), scatter_dimension=0, tiled=True),
        lax.psum_scatter(output_term, ("grp", "ctx", "wsh"), scatter_dimension=0, tiled=True),
        lax.psum_scatter(gain_term, ("grp", "ctx", "wsh"), scatter_dimension=0, tiled=True),
        lax.psum_scatter(centroid_term, ("grp", "ctx", "wsh"), scatter_dimension=1, tiled=True),
    )
    return (
        output.astype(jnp.bfloat16)[None],
        input_grad[None],
        gain_grad,
        project_grad,
        output_grad,
        centroid_grad,
        up_grad_out,
        down_grad_out,
    )


def solution(mesh):
    placed = (
        P(("grp", "wsh"), "ctx", None),
        P(("grp", "wsh"), "ctx", None),
        P(("grp", "ctx", "wsh")),
        P(("grp", "ctx", "wsh"), None),
        P(("grp", "ctx", "wsh"), None),
        P(None, ("grp", "ctx", "wsh")),
        P("ctx", None, "grp", "wsh"),
        P("ctx", None, "wsh", "grp"),
        P(("grp", "wsh"), None),
        P(("grp", "wsh"), None),
        P(("grp", "wsh"), "ctx", None),
    )
    return jax.shard_map(
        shards,
        mesh=mesh,
        in_specs=placed,
        out_specs=(
            P(("grp", "wsh"), "ctx", None),
            P(("grp", "wsh"), "ctx", None),
            P(("grp", "ctx", "wsh")),
            P(("grp", "ctx", "wsh"), None),
            P(("grp", "ctx", "wsh"), None),
            P(None, ("grp", "ctx", "wsh")),
            P("ctx", None, "grp", "wsh"),
            P("ctx", None, "wsh", "grp"),
        ),
        check_vma=False,
    )
```

profile of v0, /device:TPU:0, one launch (start us, length us, event | category | flops | bytes accessed | tf_op | source)
XLA Modules:
  0.0 1154.2 jit_solution(15831417605486393407)
XLA Ops:
  8.8 42.4 %all-reduce = bf16[1024]{0:T(1024)(128)(2,1)S(1)} all-reduce(bf16[1024]{0:T(1024)(128)(2,1)S(1)} %dynamic-update-slice), channel_id=1, replica_groups=mesh['grp'=4,'ctx'=2,'wsh'=4] {'grp','ctx','wsh'}, use_global_device_ids=true, to_apply=%add | all-reduce | flops 1024 | bytes 4096
  53.5 29.9 %all-gather.11.cloned.1.call-done = bf16[1024,3072]{1,0:T(8,128)(2,1)} async-done(((bf16[32,3072]{1,0:T(8,128)(2,1)}), bf16[1024,3072]{1,0:T(8,128)(2,1)}) %all-gather.11.cloned.1.call-update) | async-done | bytes 6291472 | tf_op jit(solution)/shard_map/all_gather | solution.py:86
  90.1 65.5 %all-gather = bf16[32,32,2]{1,2,0:T(2,128)(2,1)S(1)} all-gather(bf16[1,32,2]{1,2,0:T(2,128)(2,1)S(1)} %bitcast.299), channel_id=1, replica_groups=mesh['grp'=4,'ctx'=2,'wsh'=4] {'grp','ctx','wsh'}, dimensions={0}, use_global_device_ids=true | all-gather | bytes 4224 | tf_op jit(solution)/shard_map/all_gather | solution.py:89
  172.4 8.6 all_to_all.20
  181.6 21.0 %all-gather.19.cloned.1.call-done = bf16[1,2,1024,1024]{3,2,1,0:T(8,128)(2,1)} async-done(((bf16[1,2,256,1024]{3,2,1,0:T(8,128)(2,1)}), bf16[1,2,1024,1024]{3,2,1,0:T(8,128)(2,1)}) %all-gather.19.cloned.1.call-update) | async-done | bytes 4194320 | tf_op jit(solution)/shard_map/all_gather | solution.py:92
  202.6 34.2 %all-gather.17.cloned.1.call-done = bf16[640,1024]{1,0:T(8,128)(2,1)} async-done(((bf16[160,1024]{1,0:T(8,128)(2,1)}), bf16[640,1024]{1,0:T(8,128)(2,1)}) %all-gather.17.cloned.1.call-update) | async-done | bytes 1310736 | tf_op jit(solution)/shard_map/all_gather | solution.py:40
  241.8 30.4 %all-gather.21.cloned.1.call-done = bf16[1,2,1024,1024]{3,2,1,0:T(8,128)(2,1)} async-done(((bf16[1,2,1024,256]{3,2,1,0:T(8,128)(2,1)}), bf16[1,2,1024,1024]{3,2,1,0:T(8,128)(2,1)}) %all-gather.21.cloned.1.call-update) | async-done | bytes 4194320 | tf_op jit(solution)/shard_map/all_gather | solution.py:93
  277.5 31.3 %reduce-scatter.15.cloned.1.call-done = bf16[160,1024]{1,0:T(8,128)(2,1)} async-done(((bf16[640,1024]{1,0:T(8,128)(2,1)}), bf16[160,1024]{1,0:T(8,128)(2,1)}) %reduce-scatter.15.cloned.1.call-update) | async-done | bytes 327696 | tf_op jit(solution)/shard_map/reduce_scatter | solution.py:44
  310.8 31.6 %all-gather.23.cloned.1.call-done = bf16[640,1024]{1,0:T(8,128)(2,1)} async-done(((bf16[160,1024]{1,0:T(8,128)(2,1)}), bf16[640,1024]{1,0:T(8,128)(2,1)}) %all-gather.23.cloned.1.call-update) | async-done | bytes 1310736 | tf_op jit(solution)/shard_map/all_gather | solution.py:40
  350.6 30.3 %reduce-scatter.17.cloned.1.call-done = bf16[160,1024]{1,0:T(8,128)(2,1)} async-done(((bf16[640,1024]{1,0:T(8,128)(2,1)}), bf16[160,1024]{1,0:T(8,128)(2,1)}) %reduce-scatter.17.cloned.1.call-update) | async-done | bytes 327696 | tf_op jit(solution)/shard_map/reduce_scatter | solution.py:44
  382.1 8.4 all_to_all.21
  392.4 8.6 all_to_all.22
  401.1 30.9 %all-gather.25.cloned.1.call-done = bf16[640,1024]{1,0:T(8,128)(2,1)} async-done(((bf16[160,1024]{1,0:T(8,128)(2,1)}), bf16[640,1024]{1,0:T(8,128)(2,1)}) %all-gather.25.cloned.1.call-update) | async-done | bytes 1310736 | tf_op jit(solution)/shard_map/all_gather | solution.py:40
  432.0 5.8 fusion.13
  441.5 30.3 %reduce-scatter.19.cloned.1.call-done = bf16[160,1024]{1,0:T(8,128)(2,1)} async-done(((bf16[640,1024]{1,0:T(8,128)(2,1)}), bf16[160,1024]{1,0:T(8,128)(2,1)}) %reduce-scatter.19.cloned.1.call-update) | async-done | bytes 327696 | tf_op jit(solution)/shard_map/reduce_scatter | solution.py:44
  473.7 31.6 %all-gather.27.cloned.1.call-done = bf16[640,1024]{1,0:T(8,128)(2,1)} async-done(((bf16[160,1024]{1,0:T(8,128)(2,1)}), bf16[640,1024]{1,0:T(8,128)(2,1)}) %all-gather.27.cloned.1.call-update) | async-done | bytes 1310736 | tf_op jit(solution)/shard_map/all_gather | solution.py:40
  505.4 5.8 fusion.6
  515.6 29.7 %reduce-scatter.21.cloned.1.call-done = bf16[160,1024]{1,0:T(8,128)(2,1)} async-done(((bf16[640,1024]{1,0:T(8,128)(2,1)}), bf16[160,1024]{1,0:T(8,128)(2,1)}) %reduce-scatter.21.cloned.1.call-update) | async-done | bytes 327696 | tf_op jit(solution)/shard_map/reduce_scatter | solution.py:44
  615.2 6.5 fusion.100
  623.5 120.6 %reduce-scatter.33.cloned.1.call-done = f32[32,2]{1,0:T(8,128)} async-done(((f32[1024,2]{1,0:T(8,128)}), f32[32,2]{1,0:T(8,128)}) %reduce-scatter.33.cloned.1.call-update) | async-done | bytes 272
  750.8 37.1 %all-reduce.1 = f32[1024]{0:T(1024)S(1)} all-reduce(f32[1024]{0:T(1024)S(1)} %get-tuple-element.8), channel_id=7, replica_groups=mesh['grp'=4,'ctx'=2,'wsh'=4] {'grp','ctx','wsh'}, use_global_device_ids=true, to_apply=%region_29.30.clone | all-reduce | flops 1024 | bytes 8192
  792.3 42.5 %reduce-scatter.29.cloned.1.call-done = bf16[1,2,1024,256]{3,2,1,0:T(8,128)(2,1)} async-done(((bf16[1,2,1024,1024]{3,2,1,0:T(8,128)(2,1)}), bf16[1,2,1024,256]{3,2,1,0:T(8,128)(2,1)}) %reduce-scatter.29.cloned.1.call-update) | async-done | bytes 1048592 | tf_op jit(solution)/shard_map/reduce_scatter | solution.py:199
  837.5 150.1 %reduce-scatter.25.cloned.1.call-done = f32[32,1024]{1,0:T(8,128)} async-done(((f32[1024,1024]{1,0:T(8,128)}), f32[32,1024]{1,0:T(8,128)}) %reduce-scatter.25.cloned.1.call-update) | async-done | bytes 131088 | tf_op jit(solution)/shard_map/reduce_scatter | solution.py:266
  987.6 159.6 %reduce-scatter.23.cloned.1.call-done = f32[32,3072]{1,0:T(8,128)} async-done(((f32[1024,3072]{1,0:T(8,128)}), f32[32,3072]{1,0:T(8,128)}) %reduce-scatter.23.cloned.1.call-update) | async-done | bytes 393232 | tf_op jit(solution)/shard_map/reduce_scatter | solution.py:265
  (323 shorter events, 145.8 us)
Async XLA Ops:
  7.2 76.2 %all-gather.11.cloned.1.call-start = ((), (), s32[]{:S(2)}) async-start(), calls=%async_computation.14 | async-start | bytes 6488064 | tf_op jit(solution)/shard_map/all_gather | solution.py:86
  7.9 149.8 %all-gather.13.cloned.1.call-start = ((), (), s32[]{:S(2)}) async-start(), calls=%async_computation.15 | async-start | bytes 1572864 | tf_op jit(solution)/shard_map/all_gather | solution.py:107
  87.4 68.4 %copy-start.46 = (s32[1,128,1]{1,2,0:T(1,128)S(1)}, s32[1,128,1]{1,2,0:T(1,128)}, u32[]{:S(2)}) copy-start(s32[1,128,1]{1,2,0:T(1,128)} %param.21) | copy-start | bytes 1540
  88.2 81.1 %all-gather.15.cloned.1.call-start = ((), (), s32[]{:S(2)}) async-start(), calls=%async_computation.16 | async-start | bytes 2162688 | tf_op jit(solution)/shard_map/all_gather | solution.py:87
  89.0 113.6 %all-gather.19.cloned.1.call-start = ((), (), s32[]{:S(2)}) async-start(), calls=%async_computation.18 | async-start | bytes 5242880 | tf_op jit(solution)/shard_map/all_gather | solution.py:92
  89.5 147.2 %all-gather.17.cloned.1.call-start = ((), (), s32[]{:S(2)}) async-start(), calls=%async_computation.17 | async-start | bytes 1638400 | tf_op jit(solution)/shard_map/all_gather | solution.py:40
  181.0 91.2 %all-gather.21.cloned.1.call-start = ((), (), s32[]{:S(2)}) async-start(), calls=%async_computation.19 | async-start | bytes 5242880 | tf_op jit(solution)/shard_map/all_gather | solution.py:93
  181.6 127.2 %reduce-scatter.15.cloned.1.call-start = ((), (), s32[]{:S(2)}) async-start(), calls=%async_computation.20 | async-start | bytes 1638400 | tf_op jit(solution)/shard_map/reduce_scatter | solution.py:44
  241.8 67.0 %copy-start.2 = (bf16[2,80,1024]{2,1,0:T(8,128)(2,1)S(1)}, bf16[2,80,1024]{2,1,0:T(8,128)(2,1)}, u32[]{:S(2)}) copy-start(bf16[2,80,1024]{2,1,0:T(8,128)(2,1)} %all_to_all.20) | copy-start | bytes 983044
  277.4 65.0 %all-gather.23.cloned.1.call-start = ((), (), s32[]{:S(2)}) async-start(), calls=%async_computation.21 | async-start | bytes 1638400 | tf_op jit(solution)/shard_map/all_gather | solution.py:40
  310.6 70.3 %reduce-scatter.17.cloned.1.call-start = ((), (), s32[]{:S(2)}) async-start(), calls=%async_computation.22 | async-start | bytes 1638400 | tf_op jit(solution)/shard_map/reduce_scatter | solution.py:44
  350.5 40.0 %copy-start.6 = (bf16[1,128,1024]{2,1,0:T(8,128)(2,1)S(1)}, bf16[1,128,1024]{2,1,0:T(8,128)(2,1)}, u32[]{:S(2)}) copy-start(bf16[1,128,1024]{2,1,0:T(8,128)(2,1)} %param.12) | copy-start | bytes 786436
  350.5 41.0 %copy-start.61 = (f32[128]{0:T(128)S(1)}, f32[128]{0:T(128)}, u32[]{:S(2)}) copy-start(f32[128]{0:T(128)} %get-tuple-element.39) | copy-start | bytes 1540
  350.5 81.4 %all-gather.25.cloned.1.call-start = ((), (), s32[]{:S(2)}) async-start(), calls=%async_computation.23 | async-start | bytes 1638400 | tf_op jit(solution)/shard_map/all_gather | solution.py:40
  401.0 70.9 %reduce-scatter.19.cloned.1.call-start = ((), (), s32[]{:S(2)}) async-start(), calls=%async_computation.24 | async-start | bytes 1638400 | tf_op jit(solution)/shard_map/reduce_scatter | solution.py:44
  441.5 63.9 %all-gather.27.cloned.1.call-start = ((), (), s32[]{:S(2)}) async-start(), calls=%async_computation.25 | async-start | bytes 1638400 | tf_op jit(solution)/shard_map/all_gather | solution.py:40
  473.7 71.6 %reduce-scatter.21.cloned.1.call-start = ((), (), s32[]{:S(2)}) async-start(), calls=%async_computation.26 | async-start | bytes 1638400 | tf_op jit(solution)/shard_map/reduce_scatter | solution.py:44
  547.1 9.4 all-to-all-start.3
  550.6 63.2 %reduce-scatter.31.cloned.1.call-start = ((), (), s32[]{:S(2)}) async-start(), calls=%async_computation.31 | async-start | bytes 1572864
  588.8 155.2 %reduce-scatter.33.cloned.1.call-start = ((), (), s32[]{:S(2)}) async-start(), calls=%async_computation.32 | async-start | bytes 540672
  590.4 199.1 %reduce-scatter.27.cloned.1.call-start = ((), (), s32[]{:S(2)}) async-start(), calls=%async_computation.29 | async-start | bytes 5242880 | tf_op jit(solution)/shard_map/reduce_scatter | solution.py:196
  598.5 236.4 %reduce-scatter.29.cloned.1.call-start = ((), (), s32[]{:S(2)}) async-start(), calls=%async_computation.30 | async-start | bytes 5242880 | tf_op jit(solution)/shard_map/reduce_scatter | solution.py:199
  608.2 379.4 %reduce-scatter.25.cloned.1.call-start = ((), (), s32[]{:S(2)}) async-start(), calls=%async_computation.28 | async-start | bytes 4325376 | tf_op jit(solution)/shard_map/reduce_scatter | solution.py:266
  611.9 535.3 %reduce-scatter.23.cloned.1.call-start = ((), (), s32[]{:S(2)}) async-start(), calls=%async_computation.27 | async-start | bytes 12976128 | tf_op jit(solution)/shard_map/reduce_scatter | solution.py:265
  (72 other events, 455.6 us)
Sparse Core Ops, SparseCore 0:
  10.9 72.4 all-gather.10
  88.4 19.8 all-gather.12
  111.2 56.5 all-gather.14
  169.2 33.3 all-gather.18
  204.0 32.6 all-gather.16
  238.2 34.0 all-gather.20
  277.5 31.2 reduce-scatter.14
  310.9 31.4 all-gather.22
  350.6 30.2 reduce-scatter.16
  401.1 30.7 all-gather.24
  441.6 30.2 reduce-scatter.18
  473.9 31.4 all-gather.26
  515.1 30.1 reduce-scatter.20
  588.9 18.4 reduce-scatter.30
  609.6 134.4 reduce-scatter.32
  746.4 41.0 reduce-scatter.26
  790.0 44.7 reduce-scatter.28
  837.5 150.0 reduce-scatter.24
  994.2 152.9 reduce-scatter.22
where the time goes:
time: 1160 us; the launch traced here: 1150 us
  waiting for transfers between devices  812 us (70%)
  blocking collectives  171 us (15%)
  matrix products  96.8 us (8%)
  other arithmetic  27.1 us (2%)
  local copies, waits for them, and re-layouts  26.8 us (2%)
  between operations  15.6 us (1%)
    reduce_scatter x1, waiting for transfers between devices, shards(): lax.psum_scatter(project_term, ('grp', 'ctx', 'wsh'), scatter_dimension=0...  160 us
    reduce_scatter x1, waiting for transfers between devices, shards(): lax.psum_scatter(output_term, ('grp', 'ctx', 'wsh'), scatter_dimension=0,...  150 us
    all_gather x4, waiting for transfers between devices, spread_rows(): return lax.all_gather(local_rows, 'wsh', axis=0, tiled=True)  128 us
    unnamed x21, waiting for transfers between devices  123 us
    reduce_scatter x4, waiting for transfers between devices, collect_rows(): lax.psum_scatter(partial_term.astype(jnp.bfloat16), 'wsh', scatter_dimens...  122 us
    unnamed x2, blocking collectives  79.5 us
    all_gather x1, blocking collectives, shards(): lax.all_gather(centroids, ('grp', 'ctx', 'wsh'), axis=1, tiled=True)  65.5 us
    reduce_scatter x1, waiting for transfers between devices, shards(): lax.psum_scatter(down_terms.astype(jnp.bfloat16), 'grp', scatter_dimensio...  42.5 us
  transfers between devices with their start and end apart: 20, of which 16 were waited for; matrix products, arithmetic and copies ran while one was open for 6% of the time, Pallas kernels for 0%

commit v1 on v0

--- a/solution.py
+++ b/solution.py
@@ -3,6 +3,8 @@
 import jax
 import jax.numpy as jnp
 from jax import lax
+from jax.experimental import pallas as pl
+from jax.experimental.pallas import tpu as pltpu
 from jax.sharding import PartitionSpec as P
 
 HEADS = 16
@@ -279,33 +281,904 @@
     )
 
 
+VMEM_LIMIT = 60 * 2**20
+
+IN_SPECS = (
+    P(("grp", "wsh"), "ctx", None),
+    P(("grp", "wsh"), "ctx", None),
+    P(("grp", "ctx", "wsh")),
+    P(("grp", "ctx", "wsh"), None),
+    P(("grp", "ctx", "wsh"), None),
+    P(None, ("grp", "ctx", "wsh")),
+    P("ctx", None, "grp", "wsh"),
+    P("ctx", None, "wsh", "grp"),
+    P(("grp", "wsh"), None),
+    P(("grp", "wsh"), None),
+    P(("grp", "wsh"), "ctx", None),
+)
+OUT_SPECS = (
+    P(("grp", "wsh"), "ctx", None),
+    P(("grp", "wsh"), "ctx", None),
+    P(("grp", "ctx", "wsh")),
+    P(("grp", "ctx", "wsh"), None),
+    P(("grp", "ctx", "wsh"), None),
+    P(None, ("grp", "ctx", "wsh")),
+    P("ctx", None, "grp", "wsh"),
+    P("ctx", None, "wsh", "grp"),
+)
+
+BF = jnp.bfloat16
+F32 = jnp.float32
+NN = ((1,), (0,))
+NT = ((1,), (1,))
+TN = ((0,), (0,))
+MESH = pl.DeviceIdType.MESH
+GELU_C = 0.7978845608028654
+EXTRA = 128
+CAP = 80
+
+
+def dot(a, b, dims=NN):
+    return lax.dot_general(a, b, (dims, ((), ())), preferred_element_type=F32)
+
+
+def gelu_both(h):
+    sq = h * h
+    t = jnp.tanh(GELU_C * h * (1.0 + 0.044715 * sq))
+    half = 0.5 * (1.0 + t)
+    slope = half + 0.5 * h * (1.0 - t * t) * (GELU_C * (1.0 + 3.0 * 0.044715 * sq))
+    return h * half, slope
+
+
+def copy_in(src, dst, sem):
+    return pltpu.make_async_copy(src, dst, sem)
+
+
+class Copies:
+    def __init__(self, send, recv):
+        self.send, self.recv, self.used = send, recv, 0
+
+    def block(self, count):
+        first = self.used
+        self.used += count
+        return first
+
+    def at(self, index, src, dst, device):
+        return pltpu.make_async_remote_copy(
+            src_ref=src,
+            dst_ref=dst,
+            send_sem=self.send.at[index],
+            recv_sem=self.recv.at[index],
+            device_id=device,
+            device_id_type=MESH,
+        )
+
+    def new(self, src, dst, device):
+        return self.at(self.block(1), src, dst, device)
+
+
+class Place:
+    def __init__(self):
+        g, y, w = lax.axis_index("grp"), lax.axis_index("ctx"), lax.axis_index("wsh")
+        self.g, self.y, self.w = g, y, w
+        self.x = lax.div(g, 2)
+        self.c = g - 2 * self.x
+        self.gx = 2 * (1 - self.x) + self.c
+        self.gc = 2 * self.x + 1 - self.c
+        self.gd = 2 * (1 - self.x) + 1 - self.c
+        self.wb = lax.rem(w, 2)
+        self.w1 = w + 1 - 2 * self.wb
+        self.w2 = lax.rem(w + 2, 4)
+        self.dev_x = (self.gx, y, w)
+        self.dev_c = (self.gc, y, w)
+        self.dev_y = (g, 1 - y, w)
+        self.dev_z = lambda k: (g, y, lax.rem(w + k, 4))
+
+    def team(self, j):
+        jx, jz = lax.rem(j, 2), lax.div(j, 2)
+        tx = self.x + jx - 2 * self.x * jx
+        tz = self.wb + jz - 2 * self.wb * jz
+        return 2 * tx + tz, (2 * tx + self.c, self.y, (1 - jz) * self.w + jz * self.w1)
+
+
+def greet(devices):
+    barrier = pltpu.get_barrier_semaphore()
+    for device in devices:
+        pl.semaphore_signal(barrier, inc=1, device_id=device, device_id_type=MESH)
+    pl.semaphore_wait(barrier, len(devices))
+
+
+def dispatch_block(route_rows, expert):
+    member = (route_rows == expert.astype(F32)).astype(F32)
+    earlier = lax.broadcasted_iota(jnp.int32, (128, 128), 0) < lax.broadcasted_iota(jnp.int32, (128, 128), 1)
+    rank = dot(member.astype(BF), earlier.astype(F32).astype(BF))
+    slot = lax.broadcasted_iota(jnp.int32, (CAP, 128), 0).astype(F32)
+    hit = (jnp.broadcast_to(rank[0:1, :], (CAP, 128)) == slot) & (
+        jnp.broadcast_to(member[0:1, :], (CAP, 128)) > 0.5
+    )
+    return hit.astype(F32).astype(BF)
+
+
+def place_of(meta, index):
+    place = jnp.where(index < 128, meta[3], meta[4]) * 128 + lax.rem(index, 128)
+    bound = meta[0]
+    sequence = jnp.where(place >= bound, 1, 0)
+    for part in (1, 2):
+        bound = bound + meta[part]
+        sequence = sequence + jnp.where(place >= bound, 1, 0)
+    return place, sequence
+
+
+def forward_kernel(
+    meta, tok, cot, rts, wq_in, wo_in, up_in, dn_in,
+    XG, QKV, PR, MXH, WQ, WO, RT, OUTS, RESS, CGR, GU1, GD1, S2U, S2D,
+    TQ, CG, XH, NRM, UP, DN, DSP, XS, GS, MS, AA,
+    R1, R2, R3, R4, RB, PS, OWN, GP1, A1, A2, DH, SUMS,
+    GU2, GD2, CRU, CRD, ZSU, ZSD, ZRU, ZRD,
+    send, recv, local,
+):
+    p = Place()
+    g, y, w, x = p.g, p.y, p.w, p.x
+    cp = Copies(send, recv)
+    greet([p.dev_x, p.dev_c, p.dev_y, p.dev_z(1), p.dev_z(2), p.dev_z(3), p.team(3)[1]])
+    nlocal = [0]
+
+    def here(src, dst):
+        nlocal[0] += 1
+        return copy_in(src, dst, local.at[nlocal[0] - 1])
+
+    def go(*items):
+        for item in items:
+            item.start()
+        return items
+
+    def wait(*items):
+        for item in items:
+            item.wait()
+
+    mine = pl.ds(y * 128, 128)
+    row = pl.ds(pl.multiple_of(g * 256 + y * 128 + w * 32, 32), 32)
+    row_o = pl.ds(pl.multiple_of(g * 128 + w * 32, 32), 32)
+    row_t = pl.ds(pl.multiple_of(w * 32, 32), 32)
+    zq = []
+    zo = []
+    for k in (1, 3, 2):
+        zq += go(
+            cp.new(wq_in.at[y], WQ.at[row, :], p.dev_z(k)),
+            cp.new(wq_in.at[1 - y], TQ.at[row_t, :], p.dev_z(k)),
+        )
+    own = go(
+        here(wq_in.at[y], WQ.at[row, :]),
+        here(wq_in.at[1 - y], TQ.at[row_t, :]),
+        here(wo_in, WO.at[y, row_o, :]),
+        here(tok, XG.at[mine, :]),
+        here(cot, CG.at[mine, :]),
+        here(rts, RT.at[y]),
+    )
+    ty = go(
+        cp.new(tok, XG.at[mine, :], p.dev_y),
+        cp.new(rts, RT.at[y], p.dev_y),
+    )
+    for k in (1, 3, 2):
+        zo += go(cp.new(wo_in, WO.at[y, row_o, :], p.dev_z(k)))
+
+    def dq(q):
+        return pl.ds(pl.multiple_of(q * 256, 256), 256)
+
+    half = pl.ds(pl.multiple_of(x * 512, 512), 512)
+    other = pl.ds(pl.multiple_of((1 - x) * 512, 512), 512)
+
+    def e_first(s):
+        return go(
+            cp.new(up_in.at[s, :, other], UP.at[s, 0, dq(g), :], p.dev_x),
+            cp.new(dn_in.at[s, other, :], DN.at[s, 0, :, dq(g)], p.dev_x),
+        )
+
+    def e_core0(s):
+        return go(
+            cp.new(up_in.at[s, :, half], UP.at[s, 0, dq(g), :], p.dev_c),
+            cp.new(dn_in.at[s, half, :], DN.at[s, 0, :, dq(g)], p.dev_c),
+        )
+
+    def e_local(s):
+        return go(
+            here(up_in.at[s, :, half], UP.at[s, 0, dq(g), :]),
+            here(dn_in.at[s, half, :], DN.at[s, 0, :, dq(g)]),
+        )
+
+    def e_z(s):
+        return go(
+            cp.new(up_in.at[s, :, half], UP.at[s, 1, dq(g), :], p.dev_z(2)),
+            cp.new(dn_in.at[s, half, :], DN.at[s, 1, :, dq(g)], p.dev_z(2)),
+        )
+
+    def e_relay(s):
+        return go(
+            cp.new(UP.at[s, 0, dq(p.gx), :], UP.at[s, 1, dq(p.gx), :], p.dev_z(2)),
+            cp.new(DN.at[s, 0, :, dq(p.gx)], DN.at[s, 1, :, dq(p.gx)], p.dev_z(2)),
+        )
+
+    def e_core(s, q, which):
+        return go(
+            cp.new(UP.at[s, q, dq(which), :], UP.at[s, q, dq(which), :], p.dev_c),
+            cp.new(DN.at[s, q, :, dq(which)], DN.at[s, q, :, dq(which)], p.dev_c),
+        )
+
+    e1 = [e_first(0)]
+    el = e_local(0) + e_local(1)
+    ec0 = [e_core0(0), e_core0(1)]
+
+    wait(*own)
+    wait(*ty)
+    cy = go(cp.new(cot, CG.at[mine, :], p.dev_y))
+    values = XG[...].astype(F32)
+    centred = values - jnp.mean(values, axis=1, keepdims=True)
+    inverse = lax.rsqrt(jnp.mean(centred * centred, axis=1, keepdims=True) + 1e-05)
+    XH[...] = centred * inverse
+    for b in (0, 1):
+        DSP[b] = dispatch_block(RT[b], y)
+        XS[b * CAP : (b + 1) * CAP, :] = dot(DSP[b], XG[b * 128 : (b + 1) * 128, :])
+
+    wait(*zq)
+    yq = go(cp.new(TQ, WQ.at[pl.ds(pl.multiple_of(g * 256 + y * 128, 128), 128), :], p.dev_y))
+    wait(*e1[0])
+    ez = [e_z(0)]
+    er = [e_relay(0)]
+    ec = [e_core(0, 0, p.gx)]
+    wait(*zo)
+    block_y = pl.ds(pl.multiple_of(g * 128, 128), 128)
+    yo = go(cp.new(WO.at[y, block_y, :], WO.at[y, block_y, :], p.dev_y))
+    wait(*yq)
+    xq = go(
+        cp.new(WQ.at[dq(g), :], WQ.at[dq(g), :], p.dev_x),
+        cp.new(WQ.at[dq(g), :], WQ.at[dq(g), :], p.dev_c),
+    )
+    wait(*yo)
+    xo = go(
+        cp.new(WO.at[:, block_y, :], WO.at[:, block_y, :], p.dev_x),
+        cp.new(WO.at[:, block_y, :], WO.at[:, block_y, :], p.dev_c),
+    )
+    e1.append(e_first(1))
+    wait(*xq)
+    fq = go(cp.new(WQ.at[dq(p.gx), :], WQ.at[dq(p.gx), :], p.dev_c))
+    wait(*cy)
+    for b in (0, 1):
+        GS[b * CAP : (b + 1) * CAP, :] = dot(DSP[b], CG[b * 128 : (b + 1) * 128, :]).astype(BF)
+    wait(*fq)
+
+    pick = (
+        lax.broadcasted_iota(jnp.int32, (8, EXTRA), 0) == lax.broadcasted_iota(jnp.int32, (8, EXTRA), 1)
+    ).astype(F32).astype(BF)
+    extra = dot(pick, WQ[:, 1536:], NT)
+    gain = extra[0:1, :]
+    centroid = jnp.where(y == 0, extra[1:2, :], extra[2:3, :])
+    NRM[...] = (XH[...] * gain).astype(BF)
+
+    def project(t, carry):
+        cols = pl.ds(pl.multiple_of(t * 512, 512), 512)
+        QKV[:, cols] = dot(NRM[...], WQ[:, cols]).astype(BF)
+        return carry
+
+    lax.fori_loop(0, 3, project, 0)
+    wait(*xo)
+    far = pl.ds(pl.multiple_of(p.gx * 128, 128), 128)
+    fo = go(cp.new(WO.at[:, far, :], WO.at[:, far, :], p.dev_c))
+
+    place_q, seq_q = place_of(meta, lax.broadcasted_iota(jnp.int32, (256, 256), 0))
+    place_k, seq_k = place_of(meta, lax.broadcasted_iota(jnp.int32, (256, 256), 1))
+    allowed = (seq_q == seq_k) & (place_k <= place_q)
+    low_half = lax.broadcasted_iota(jnp.int32, (256, 128), 1) < 64
+    mixed_first = cp.block(4)
+
+    def mixed_copy(t):
+        cols = pl.ds(pl.multiple_of(t * 128, 128), 128)
+        return cp.at(mixed_first + t, MXH.at[y, :, cols], MXH.at[y, :, cols], p.dev_y)
+
+    def heads(t, carry):
+        cols = pl.ds(pl.multiple_of(t * 128, 128), 128)
+        q2 = QKV[:, cols]
+        k2 = QKV[:, pl.ds(pl.multiple_of(512 + t * 128, 128), 128)]
+        v2 = QKV[:, pl.ds(pl.multiple_of(1024 + t * 128, 128), 128)]
+        parts = []
+        for i in (0, 1):
+            keep = low_half if i == 0 else ~low_half
+            scores = dot(jnp.where(keep, q2, jnp.zeros_like(q2)), k2, NT) * 0.125
+            scores = jnp.where(allowed, scores, -1000000000.0)
+            exponent = jnp.exp(scores - jnp.max(scores, axis=1, keepdims=True))
+            probs = exponent / jnp.sum(exponent, axis=1, keepdims=True)
+            PR[2 * t + i] = probs
+            parts.append(dot(probs.astype(BF), v2))
+        MXH[y, :, cols] = jnp.where(low_half, parts[0], parts[1]).astype(BF)
+        mixed_copy(t).start()
+        return carry
+
+    lax.fori_loop(0, 4, heads, 0)
+
+    def mixed_pick(yy):
+        for b in (0, 1):
+            MS[yy, b * CAP : (b + 1) * CAP, :] = dot(DSP[b], MXH[yy, b * 128 : (b + 1) * 128, :]).astype(BF)
+
+    mixed_pick(y)
+    wait(*fo)
+    AA[...] = XS[...] + dot(MS[y], WO[y])
+    lax.fori_loop(0, 4, lambda t, carry: (mixed_copy(t).wait(), carry)[1], 0)
+    mixed_pick(1 - y)
+    AA[...] += dot(MS[1 - y], WO[1 - y])
+    gate = jax.nn.sigmoid(jnp.sum(AA[...] * centroid, axis=1, keepdims=True))
+
+    wait(*el)
+    me = pl.ds(pl.multiple_of(p.team(0)[0] * 160, 160), 160)
+
+    def spread(first, R):
+        def one(j):
+            device = p.team(j)[1]
+            return cp.at(first + j - 1, R.at[me, :], R.at[me, :], device)
+
+        return one
+
+    def each(fn):
+        def body(j, carry):
+            fn(j)
+            return carry
+
+        lax.fori_loop(1, 4, body, 0)
+
+    def reduce_copy(first, k, b):
+        def one(j):
+            device = p.team(j)[1]
+            return cp.at(first + j - 1, PS.at[k, j - 1], RB.at[b, j - 1], device)
+
+        return one
+
+    firsts = [cp.block(3) for _ in range(8)]
+    g1, g2, g3, g4 = (spread(f, R) for f, R in zip(firsts[:4], (R1, R2, R3, R4)))
+    r1, r3, r2, r4 = (reduce_copy(f, k, b) for f, k, b in zip(firsts[4:], (0, 1, 2, 0), (0, 1, 2, 3)))
+
+    def rows_of(j):
+        return pl.ds(pl.multiple_of(p.team(j)[0] * 160, 160), 160)
+
+    R1[me, :] = AA[...].astype(BF)
+    each(lambda j: g1(j).start())
+    R3[me, :] = (gate * GS[...].astype(F32)).astype(BF)
+    each(lambda j: g3(j).start())
+
+    wait(*ec0[0])
+    wait(*ec[0])
+    wait(*ez[0])
+    ec1 = e_core(0, 1, g)
+    wait(*er[0])
+    ec2 = e_core(0, 1, p.gx)
+    wait(*e1[1])
+    ez.append(e_z(1))
+    er.append(e_relay(1))
+    ec.append(e_core(1, 0, p.gx))
+    wait(*ec1)
+    wait(*ec2)
+
+    def cols_of(q):
+        return slice(q * 512, (q + 1) * 512)
+
+    def first_forward(j):
+        at = rows_of(j)
+        total = None
+        for q in (0, 1):
+            active, slope = gelu_both(dot(R1[at, :], UP[0, q]))
+            GP1[at, cols_of(q)] = slope
+            A1[at, cols_of(q)] = active.astype(BF)
+            term = dot(active.astype(BF), DN[0, q])
+            total = term if total is None else total + term
+        return total
+
+    OWN[0] = first_forward(0)
+
+    def step_one(j):
+        g1(j).wait()
+        PS[0, j - 1] = first_forward(j).astype(BF)
+        r1(j).start()
+
+    each(step_one)
+    each(lambda j: r1(j).wait())
+    branch_one = OWN[0] + RB[0, 0].astype(F32) + RB[0, 1].astype(F32) + RB[0, 2].astype(F32)
+    SUMS[0] = branch_one
+    R2[me, :] = (AA[...].astype(BF).astype(F32) + branch_one).astype(BF)
+    each(lambda j: g2(j).start())
+    each(lambda j: g3(j).wait())
+
+    wait(*ec0[1])
+    wait(*ec[1])
+    wait(*ez[1])
+    ec1 = e_core(1, 1, g)
+    wait(*er[1])
+    ec2 = e_core(1, 1, p.gx)
+    wait(*ec1)
+    wait(*ec2)
+
+    def second_both(j):
+        at = rows_of(j)
+        total, total_grad = None, None
+        for q in (0, 1):
+            active, slope = gelu_both(dot(R2[at, :], UP[1, q]))
+            A2[at, cols_of(q)] = active.astype(BF)
+            grad = (slope * dot(R3[at, :], DN[1, q], NT)).astype(BF)
+            DH[at, cols_of(q)] = grad
+            term = dot(grad, UP[1, q], NT)
+            total_grad = term if total_grad is None else total_grad + term
+        for q in (0, 1):
+            term = dot(A2[at, cols_of(q)], DN[1, q])
+            total = term if total is None else total + term
+        return total, total_grad
+
+    OWN[1], OWN[2] = second_both(0)
+
+    def step_two(j):
+        g2(j).wait()
+        total, total_grad = second_both(j)
+        PS[1, j - 1] = total_grad.astype(BF)
+        r3(j).start()
+        PS[2, j - 1] = total.astype(BF)
+        r2(j).start()
+
+    each(step_two)
+
+    def weight_grads(A, R, RG, GU, GD):
+        def one(q, d):
+            qcols = pl.ds(pl.multiple_of(q * 512, 512), 512)
+            GU[q, d] = dot(R[:, dq(d)], DH[:, qcols], TN).astype(BF)
+            GD[q, d] = dot(A[:, qcols], RG[:, dq(d)], TN).astype(BF)
+
+        def body(t, carry):
+            q, k = lax.rem(t, 2), lax.div(t, 2)
+            d = lax.rem(k, 2)
+            mine_c = lax.div(k, 2)
+            cc = p.c * mine_c + (1 - p.c) * (1 - mine_c)
+            one(q, 2 * d + cc)
+            return carry
+
+        return body
+
+    body2 = weight_grads(A2, R2, R3, GU2, GD2)
+    lax.fori_loop(0, 4, body2, 0)
+    f0 = []
+    for k, (theirs, mine_d) in enumerate(((p.gc, 0), (p.gd, 1))):
+        f0 += go(
+            cp.new(GU2.at[:, theirs], CRU.at[:, k], p.dev_c),
+            cp.new(GD2.at[:, theirs], CRD.at[:, k], p.dev_c),
+        )
+    lax.fori_loop(4, 8, body2, 0)
+
+    each(lambda j: r3(j).wait())
+    middle_grad = OWN[2] + RB[1, 0].astype(F32) + RB[1, 1].astype(F32) + RB[1, 2].astype(F32)
+    SUMS[1] = middle_grad
+    R4[me, :] = (R3[me, :].astype(F32) + middle_grad).astype(BF)
+    each(lambda j: g4(j).start())
+    wait(*f0)
+    f1 = []
+    for k, d in enumerate((g, p.gx)):
+        ZSU[k] = (GU2[1, d].astype(F32) + CRU[1, k].astype(F32)).astype(BF)
+        ZSD[k] = (GD2[1, d].astype(F32) + CRD[1, k].astype(F32)).astype(BF)
+        f1 += go(
+            cp.new(ZSU.at[k], ZRU.at[k], p.dev_z(2)),
+            cp.new(ZSD.at[k], ZRD.at[k], p.dev_z(2)),
+        )
+
+    each(lambda j: r2(j).wait())
+    branch_two = OWN[1] + RB[2, 0].astype(F32) + RB[2, 1].astype(F32) + RB[2, 2].astype(F32)
+    returned = (SUMS[0] + branch_two).astype(BF).astype(F32)
+    upstream = GS[...].astype(F32)
+    OUTS[...] = (AA[...] + gate * returned).astype(BF)
+    score_grad = jnp.sum(upstream * returned, axis=1, keepdims=True) * gate * (1.0 - gate)
+    CGR[...] = jnp.broadcast_to(jnp.sum(score_grad * AA[...], axis=0, keepdims=True), CGR.shape)
+    OWN[1] = upstream + score_grad * centroid
+
+    def first_backward(j):
+        at = rows_of(j)
+        total = None
+        for q in (0, 1):
+            grad = (GP1[at, cols_of(q)] * dot(R4[at, :], DN[0, q], NT)).astype(BF)
+            DH[at, cols_of(q)] = grad
+            term = dot(grad, UP[0, q], NT)
+            total = term if total is None else total + term
+        return total
+
+    OWN[0] = first_backward(0)
+
+    def step_three(j):
+        g4(j).wait()
+        PS[0, j - 1] = first_backward(j).astype(BF)
+        r4(j).start()
+
+    each(step_three)
+    lax.fori_loop(0, 8, weight_grads(A1, R1, R4, GU1, GD1), 0)
+    each(lambda j: r4(j).wait())
+    arrived = (
+        OWN[0] + RB[3, 0].astype(F32) + RB[3, 1].astype(F32) + RB[3, 2].astype(F32) + SUMS[1]
+    ).astype(BF)
+    RESS[...] = (OWN[1] + arrived.astype(F32)).astype(BF)
+
+    wait(*f1)
+    for k, d in enumerate((g, p.gx)):
+        S2U[k] = GU2[0, d].astype(F32) + CRU[0, k].astype(F32) + ZRU[k].astype(F32)
+        S2D[k] = GD2[0, d].astype(F32) + CRD[0, k].astype(F32) + ZRD[k].astype(F32)
+
+
+def backward_kernel(
+    XG, QKV, PR, MXH, WQ, WO, RT, OUTS, RESS, CGR, GU, GD, S2U, S2D,
+    out, tgrad, pgrad, ograd, egrad, ugrad, dgrad,
+    RP, OP, RL, XH, NRM, MG, DQ, NG, NGS, NGR,
+    CRU, CRD, ZSU, ZSD, ZRU, ZRD, XSU, XSD, XRU, XRD,
+    PW, PC, PXS, PXR, PYS, PYR, PK, PZR,
+    OW, OC, OXS, OXR, OK, OZR,
+    send, recv,
+):
+    p = Place()
+    g, y, w, x = p.g, p.y, p.w, p.x
+    cp = Copies(send, recv)
+    greet([p.dev_x, p.dev_c, p.dev_y, p.dev_z(1), p.dev_z(2), p.dev_z(3)])
+
+    def go(*items):
+        for item in items:
+            item.start()
+        return items
+
+    def wait(*items):
+        for item in items:
+            item.wait()
+
+    own_slots = pl.ds(pl.multiple_of(y * CAP, 16), CAP)
+    peer_slots = pl.ds(pl.multiple_of((1 - y) * CAP, 16), CAP)
+    ry = go(cp.new(RESS, RP, p.dev_y))
+    oy = go(cp.new(OUTS.at[peer_slots, :], OP, p.dev_y))
+
+    f0 = []
+    for k, theirs in enumerate((p.gc, p.gd)):
+        f0 += go(
+            cp.new(GU.at[:, theirs], CRU.at[:, k], p.dev_c),
+            cp.new(GD.at[:, theirs], CRD.at[:, k], p.dev_c),
+        )
+    XSU[1] = S2U[1].astype(BF)
+    XSD[1] = S2D[1].astype(BF)
+    f2 = {1: go(cp.new(XSU.at[1], XRU.at[1], p.dev_x), cp.new(XSD.at[1], XRD.at[1], p.dev_x))}
+
+    half = pl.ds(pl.multiple_of(x * 512, 512), 512)
+    other = pl.ds(pl.multiple_of((1 - x) * 512, 512), 512)
+    ugrad[1, :, half] = S2U[0]
+    dgrad[1, half, :] = S2D[0]
+
+    values = XG[...].astype(F32)
+    centred = values - jnp.mean(values, axis=1, keepdims=True)
+    inverse = lax.rsqrt(jnp.mean(centred * centred, axis=1, keepdims=True) + 1e-05)
+    XH[...] = centred * inverse
+    pick = (
+        lax.broadcasted_iota(jnp.int32, (8, EXTRA), 0) == lax.broadcasted_iota(jnp.int32, (8, EXTRA), 1)
+    ).astype(F32).astype(BF)
+    gain = dot(pick, WQ[:, 1536:], NT)[0:1, :]
+    NRM[...] = (XH[...] * gain).astype(BF)
+
+    wait(*f0)
+    f1 = []
+    for k, d in enumerate((g, p.gx)):
+        ZSU[k] = (GU[1, d].astype(F32) + CRU[1, k].astype(F32)).astype(BF)
+        ZSD[k] = (GD[1, d].astype(F32) + CRD[1, k].astype(F32)).astype(BF)
+        f1 += go(
+            cp.new(ZSU.at[k], ZRU.at[k], p.dev_z(2)),
+            cp.new(ZSD.at[k], ZRD.at[k], p.dev_z(2)),
+        )
+
+    wait(*ry)
+    for b in (0, 1):
+        slots = slice(b * CAP, (b + 1) * CAP)
+        RL[b * 128 : (b + 1) * 128, :] = (
+            dot(dispatch_block(RT[b], y), RESS[slots, :], TN)
+            + dot(dispatch_block(RT[b], 1 - y), RP[slots, :], TN)
+        ).astype(BF)
+    MG[...] = dot(RL[...], WO[y], NT).astype(BF)
+
+    def rows4(d):
+        return pl.ds(pl.multiple_of(d * 128, 128), 128)
+
+    def out_rows(d):
+        OW[rows4(d), :] = dot(MXH[y, :, rows4(d)], RL[...], TN).astype(BF)
+
+    for d in (p.gc, p.gd, g, p.gx):
+        out_rows(d)
+    oc = []
+    for k, theirs in enumerate((p.gc, p.gd)):
+        oc += go(cp.new(OW.at[rows4(theirs), :], OC.at[k], p.dev_c))
+
+    low_half = lax.broadcasted_iota(jnp.int32, (256, 128), 1) < 64
+
+    def heads(t, carry):
+        c0 = pl.ds(pl.multiple_of(t * 128, 128), 128)
+        c1 = pl.ds(pl.multiple_of(512 + t * 128, 128), 128)
+        c2 = pl.ds(pl.multiple_of(1024 + t * 128, 128), 128)
+        q2, k2, v2, m2 = QKV[:, c0], QKV[:, c1], QKV[:, c2], MG[:, c0]
+        parts = []
+        for i in (0, 1):
+            keep = low_half if i == 0 else ~low_half
+            probs = PR[2 * t + i]
+            probs_grad = dot(jnp.where(keep, m2, jnp.zeros_like(m2)), v2, NT)
+            delta = jnp.sum(probs_grad * probs, axis=1, keepdims=True)
+            scores_grad = (probs * (probs_grad - delta)).astype(BF)
+            parts.append(
+                (
+                    dot(scores_grad, k2) * 0.125,
+                    dot(scores_grad, q2, TN) * 0.125,
+                    dot(probs.astype(BF), m2, TN),
+                )
+            )
+        DQ[:, c0] = jnp.where(low_half, parts[0][0], parts[1][0]).astype(BF)
+        DQ[:, c1] = jnp.where(low_half, parts[0][1], parts[1][1]).astype(BF)
+        DQ[:, c2] = jnp.where(low_half, parts[0][2], parts[1][2]).astype(BF)
+        return carry
+
+    lax.fori_loop(0, 4, heads, 0)
+
+    NG[...] = dot(DQ[...], WQ[:, :1536], NT)
+    NGS[...] = NG[pl.ds(pl.multiple_of((1 - y) * 128, 128), 128), :].astype(BF)
+    ny = go(cp.new(NGS, NGR, p.dev_y))
+    gain_row = jnp.sum(NG[...] * XH[...], axis=0, keepdims=True)
+
+    line = lax.broadcasted_iota(jnp.int32, (8, 1024), 0)
+    stack = jnp.where(line == 0, gain_row, jnp.where(line == 1 + y, CGR[0:1, :], 0.0)).astype(BF)
+
+    def dq(d):
+        return pl.ds(pl.multiple_of(d * 256, 256), 256)
+
+    def weight_rows(d):
+        PW[dq(d), :1536] = dot(NRM[:, dq(d)], DQ[...], TN).astype(BF)
+
+    def weight_loop(t, carry):
+        d, cc = lax.rem(t, 2), lax.div(t, 2)
+        weight_rows(2 * d + (p.c * cc + (1 - p.c) * (1 - cc)))
+        return carry
+
+    PW[:, 1536:] = dot(stack, pick, TN).astype(BF)
+    lax.fori_loop(0, 2, weight_loop, 0)
+    pc = []
+    for k, theirs in enumerate((p.gc, p.gd)):
+        pc += go(cp.new(PW.at[dq(theirs), :], PC.at[k], p.dev_c))
+    lax.fori_loop(2, 4, weight_loop, 0)
+
+    wait(*oc)
+    OXS[...] = (OW[rows4(p.gx), :].astype(F32) + OC[1].astype(F32)).astype(BF)
+    ox = go(cp.new(OXS, OXR, p.dev_x))
+    wait(*pc)
+    PXS[...] = (PW[dq(p.gx), :].astype(F32) + PC[1].astype(F32)).astype(BF)
+    px = go(cp.new(PXS, PXR, p.dev_x))
+
+    wait(*ny)
+    own_rows = pl.ds(pl.multiple_of(y * 128, 128), 128)
+    normed = XH[own_rows, :]
+    mine = XG[own_rows, :].astype(F32)
+    mine = mine - jnp.mean(mine, axis=1, keepdims=True)
+    inverse = lax.rsqrt(jnp.mean(mine * mine, axis=1, keepdims=True) + 1e-05)
+    scaled = (NG[own_rows, :] + NGR[...].astype(F32)) * gain
+    tgrad[...] = RL[own_rows, :].astype(F32) + inverse * (
+        scaled
+        - jnp.mean(scaled, axis=1, keepdims=True)
+        - normed * jnp.mean(scaled * normed, axis=1, keepdims=True)
+    )
+    wait(*oy)
+    route_own = RT[y]
+    out[...] = (
+        dot(dispatch_block(route_own, y), OUTS[own_slots, :], TN)
+        + dot(dispatch_block(route_own, 1 - y), OP[...], TN)
+    ).astype(BF)
+
+    wait(*ox)
+    OK[...] = (OW[rows4(g), :].astype(F32) + OC[0].astype(F32) + OXR[...].astype(F32)).astype(BF)
+
+    def row32(v):
+        return pl.ds(pl.multiple_of(v * 32, 32), 32)
+
+    oz = []
+    for k in (1, 3, 2):
+        oz += go(cp.new(OK.at[row32(lax.rem(w + k, 4)), :], OZR.at[k - 1], p.dev_z(k)))
+    wait(*px)
+
+    def summed(part):
+        rows = pl.ds(pl.multiple_of(part * 128, 128), 128)
+        full = pl.ds(pl.multiple_of(g * 256 + part * 128, 128), 128)
+        total = PW[full, :].astype(F32) + PC[0, rows, :].astype(F32) + PXR[rows, :].astype(F32)
+        return total.astype(BF)
+
+    PYS[...] = summed(1 - y)
+    py = go(cp.new(PYS, PYR, p.dev_y))
+    PK[...] = summed(y)
+    pz = []
+    for k in (1, 3, 2):
+        pz += go(cp.new(PK.at[row32(lax.rem(w + k, 4)), :], PZR.at[k - 1, 0], p.dev_z(k)))
+    wait(*py)
+    for k in (1, 3, 2):
+        pz += go(cp.new(PYR.at[row32(lax.rem(w + k, 4)), :], PZR.at[k - 1, 1], p.dev_z(k)))
+
+    wait(*f1)
+    ugrad[0, :, half] = GU[0, g].astype(F32) + CRU[0, 0].astype(F32) + ZRU[0].astype(F32)
+    dgrad[0, half, :] = GD[0, g].astype(F32) + CRD[0, 0].astype(F32) + ZRD[0].astype(F32)
+    XSU[0] = (GU[0, p.gx].astype(F32) + CRU[0, 1].astype(F32) + ZRU[1].astype(F32)).astype(BF)
+    XSD[0] = (GD[0, p.gx].astype(F32) + CRD[0, 1].astype(F32) + ZRD[1].astype(F32)).astype(BF)
+    f2[0] = go(cp.new(XSU.at[0], XRU.at[0], p.dev_x), cp.new(XSD.at[0], XRD.at[0], p.dev_x))
+    for s in (1, 0):
+        wait(*f2[s])
+        ugrad[s, :, other] = XRU[s].astype(F32)
+        dgrad[s, other, :] = XRD[s].astype(F32)
+
+    wait(*oz)
+    own32 = row32(w)
+    ograd[...] = (
+        OK[own32, :].astype(F32) + OZR[0].astype(F32) + OZR[1].astype(F32) + OZR[2].astype(F32)
+    )
+    wait(*pz)
+    sums = []
+    for i, kept in enumerate((PK, PYR)):
+        sums.append(
+            kept[own32, :].astype(F32)
+            + PZR[0, i].astype(F32)
+            + PZR[1, i].astype(F32)
+            + PZR[2, i].astype(F32)
+        )
+    pgrad[y] = sums[0][:, :1536]
+    pgrad[1 - y] = sums[1][:, :1536]
+    egrad[...] = sums[0][:, 1536:] + sums[1][:, 1536:]
+
+
+def vmem(shape, dtype=BF):
+    return pltpu.VMEM(shape, dtype)
+
+
+def fast_shards(
+    tokens, cotangent, norm_gain, project_weight, output_weight, centroids,
+    expert_up, expert_down, sequence_lengths, block_order, routes,
+):
+    in_vmem = pl.BlockSpec(memory_space=pltpu.VMEM)
+    in_any = pl.BlockSpec(memory_space=pl.ANY)
+    in_smem = pl.BlockSpec(memory_space=pltpu.SMEM)
+    shape = jax.ShapeDtypeStruct
+    extra = jnp.concatenate(
+        [norm_gain[:, None], centroids.T, jnp.zeros((32, EXTRA - 3), BF)], axis=1
+    )
+    by_plane = project_weight.reshape(32, 3, 4, 2, 128).transpose(3, 0, 1, 2, 4).reshape(2, 32, 1536)
+    wq = jnp.concatenate([by_plane, jnp.broadcast_to(extra[None], (2, 32, EXTRA))], axis=2)
+    meta = jnp.concatenate([sequence_lengths[0], block_order[0]])
+    rts = jnp.broadcast_to(routes[0, :, 0].astype(F32)[None, :], (8, 128))
+    mid_shapes = [
+        ((256, 1024), BF),
+        ((256, 1536), BF),
+        ((8, 256, 256), F32),
+        ((2, 256, 512), BF),
+        ((1024, 1536 + EXTRA), BF),
+        ((2, 512, 1024), BF),
+        ((2, 8, 128), F32),
+        ((160, 1024), BF),
+        ((160, 1024), BF),
+        ((8, 1024), F32),
+        ((2, 4, 256, 512), BF),
+        ((2, 4, 512, 256), BF),
+        ((2, 256, 512), F32),
+        ((2, 512, 256), F32),
+    ]
+    mid = pl.pallas_call(
+        forward_kernel,
+        name="forward",
+        out_shape=[shape(*s) for s in mid_shapes],
+        in_specs=[in_smem] + [in_vmem] * 5 + [in_any] * 2,
+        out_specs=[in_vmem] * len(mid_shapes),
+        scratch_shapes=[
+            vmem((128, 1536 + EXTRA)),
+            vmem((256, 1024)),
+            vmem((256, 1024), F32),
+            vmem((256, 1024)),
+            vmem((2, 2, 1024, 512)),
+            vmem((2, 2, 512, 1024)),
+            vmem((2, CAP, 128)),
+            vmem((160, 1024), F32),
+            vmem((160, 1024)),
+            vmem((2, 160, 512)),
+            vmem((160, 1024), F32),
+        ]
+        + [vmem((640, 1024))] * 4
+        + [
+            vmem((4, 3, 160, 1024)),
+            vmem((3, 3, 160, 1024)),
+            vmem((3, 160, 1024), F32),
+            vmem((640, 1024), F32),
+            vmem((640, 1024)),
+            vmem((640, 1024)),
+            vmem((640, 1024)),
+            vmem((2, 160, 1024), F32),
+            vmem((2, 4, 256, 512)),
+            vmem((2, 4, 512, 256)),
+            vmem((2, 2, 256, 512)),
+            vmem((2, 2, 512, 256)),
+            vmem((2, 256, 512)),
+            vmem((2, 512, 256)),
+            vmem((2, 256, 512)),
+            vmem((2, 512, 256)),
+            pltpu.SemaphoreType.DMA((96,)),
+            pltpu.SemaphoreType.DMA((96,)),
+            pltpu.SemaphoreType.DMA((12,)),
+        ],
+        compiler_params=pltpu.CompilerParams(
+            collective_id=0, has_side_effects=True, vmem_limit_bytes=VMEM_LIMIT
+        ),
+    )(meta, tokens[0], cotangent[0], rts, wq, output_weight, expert_up[0], expert_down[0])
+    out_shapes = [
+        ((128, 1024), BF),
+        ((128, 1024), F32),
+        ((2, 32, 1536), F32),
+        ((32, 1024), F32),
+        ((32, EXTRA), F32),
+        ((2, 256, 1024), F32),
+        ((2, 1024, 256), F32),
+    ]
+    out, tgrad, pgrad, ograd, egrad, ugrad, dgrad = pl.pallas_call(
+        backward_kernel,
+        name="backward",
+        out_shape=[shape(*s) for s in out_shapes],
+        in_specs=[in_vmem] * len(mid_shapes),
+        out_specs=[in_vmem] * len(out_shapes),
+        scratch_shapes=[
+            vmem((160, 1024)),
+            vmem((CAP, 1024)),
+            vmem((256, 1024)),
+            vmem((256, 1024), F32),
+            vmem((256, 1024)),
+            vmem((256, 512)),
+            vmem((256, 1536)),
+            vmem((256, 1024), F32),
+            vmem((128, 1024)),
+            vmem((128, 1024)),
+            vmem((2, 2, 256, 512)),
+            vmem((2, 2, 512, 256)),
+            vmem((2, 256, 512)),
+            vmem((2, 512, 256)),
+            vmem((2, 256, 512)),
+            vmem((2, 512, 256)),
+            vmem((2, 256, 512)),
+            vmem((2, 512, 256)),
+            vmem((2, 256, 512)),
+            vmem((2, 512, 256)),
+            vmem((1024, 1536 + EXTRA)),
+            vmem((2, 256, 1536 + EXTRA)),
+            vmem((256, 1536 + EXTRA)),
+            vmem((256, 1536 + EXTRA)),
+            vmem((128, 1536 + EXTRA)),
+            vmem((128, 1536 + EXTRA)),
+            vmem((128, 1536 + EXTRA)),
+            vmem((3, 2, 32, 1536 + EXTRA)),
+            vmem((512, 1024)),
+            vmem((2, 128, 1024)),
+            vmem((128, 1024)),
+            vmem((128, 1024)),
+            vmem((128, 1024)),
+            vmem((3, 32, 1024)),
+            pltpu.SemaphoreType.DMA((48,)),
+            pltpu.SemaphoreType.DMA((48,)),
+        ],
+        compiler_params=pltpu.CompilerParams(
+            collective_id=1, has_side_effects=True, vmem_limit_bytes=VMEM_LIMIT
+        ),
+    )(*mid)
+    project_grad = pgrad.reshape(2, 32, 3, 4, 128).transpose(1, 2, 3, 0, 4).reshape(32, 3072)
+    return (
+        out[None],
+        tgrad[None],
+        egrad[:, 0],
+        project_grad,
+        ograd,
+        egrad[:, 1:3].T,
+        ugrad[None],
+        dgrad[None],
+    )
+
+
 def solution(mesh):
-    placed = (
-        P(("grp", "wsh"), "ctx", None),
-        P(("grp", "wsh"), "ctx", None),
-        P(("grp", "ctx", "wsh")),
-        P(("grp", "ctx", "wsh"), None),
-        P(("grp", "ctx", "wsh"), None),
-        P(None, ("grp", "ctx", "wsh")),
-        P("ctx", None, "grp", "wsh"),
-        P("ctx", None, "wsh", "grp"),
-        P(("grp", "wsh"), None),
-        P(("grp", "wsh"), None),
-        P(("grp", "wsh"), "ctx", None),
-    )
+    sizes = dict(mesh.shape)
+    fast = sizes == {"grp": 4, "ctx": 2, "wsh": 4}
     return jax.shard_map(
-        shards,
+        fast_shards if fast else shards,
         mesh=mesh,
-        in_specs=placed,
-        out_specs=(
-            P(("grp", "wsh"), "ctx", None),
-            P(("grp", "wsh"), "ctx", None),
-            P(("grp", "ctx", "wsh")),
-            P(("grp", "ctx", "wsh"), None),
-            P(("grp", "ctx", "wsh"), None),
-            P(None, ("grp", "ctx", "wsh")),
-            P("ctx", None, "grp", "wsh"),
-            P("ctx", None, "wsh", "grp"),
-        ),
+        in_specs=IN_SPECS,
+        out_specs=OUT_SPECS,
         check_vma=False,
     )

time: 1160 us -> 379 us (0.33)
  waiting for transfers between devices: 812 us -> 0 us
  Pallas kernels: 0 us -> 360 us
  blocking collectives: 171 us -> 0 us
  matrix products: 96.8 us -> 0 us
  other arithmetic: 27.1 us -> 2.69 us
  between operations: 15.6 us -> 0.71 us
    reduce_scatter x8 -> x0, waiting for transfers between devices: 474 us -> none  [the longest x1 160 us: shards(): lax.psum_scatter(project_term, ('grp', 'ctx', 'wsh'), scatter_dimension=0...]
    pallas_call x0 -> x2, Pallas kernels: none -> 360 us  [the longest x1 268 us: fast_shards(): pl.pallas_call(forward_kernel, name='forward', out_shape=[shape(*s) for s...]
    all_gather x9 -> x0, waiting for transfers between devices: 210 us -> none  [the longest x4 128 us: spread_rows(): return lax.all_gather(local_rows, 'wsh', axis=0, tiled=True)]
    unnamed x21 -> x0, waiting for transfers between devices: 123 us -> none
    dot_general x47 -> x0, matrix products: 95.3 us -> none  [the longest x4 8.99 us: shards(): jnp.einsum('tgd,sgd->gts', head_grad, head_value, preferred_element_type=...]
    unnamed x2 -> x0, blocking collectives: 79.5 us -> none
    all_gather x1 -> x0, blocking collectives: 65.5 us -> none  [shards(): lax.all_gather(centroids, ('grp', 'ctx', 'wsh'), axis=1, tiled=True)]
    all_to_all x3 -> x0, blocking collectives: 25.6 us -> none  [trade_rows(): lax.all_to_all(shaped, 'ctx', split_axis=0, concat_axis=0, tiled=True)]
  transfers between devices with their start and end apart: 20 -> 0, of which waited for: 16 -> 0; matrix products, arithmetic and copies ran while one was open for 6% -> 0% of each run, Pallas kernels for 0% -> 0%
where the time goes in v1:
time: 379 us
  Pallas kernels  360 us (95%)
  local copies, waits for them, and re-layouts  15.6 us (4%)
    pallas_call x1, Pallas kernels, fast_shards(): pl.pallas_call(forward_kernel, name='forward', out_shape=[shape(*s) for s...  268 us
    pallas_call x1, Pallas kernels, fast_shards(): pl.pallas_call(backward_kernel, name='backward', out_shape=[shape(*s) for...  92.3 us

profile of v1, /device:TPU:0, one launch (start us, length us, event | category | flops | bytes accessed | tf_op | source)
XLA Modules:
  0.0 379.1 jit_solution(7237982449541607880)
XLA Ops:
  0.6 1.3 pad_add_fusion.meta
  1.9 0.7 convert_bitcast_fusion
  2.6 0.1 pad.4.clone
  2.6 0.6 broadcast_in_dim.30.rts
  3.2 0.7 copy.25
  4.0 0.8 copy.26
  4.7 0.1 maximum_maximum_fusion
  4.8 1.0 reshape.35
  5.9 0.1 reshape.36
  6.0 0.7 pad_maximum_fusion.wq_in
  6.7 267.7 %forward.1 = (bf16[256,1024]{1,0:T(8,128)(2,1)}, bf16[256,1536]{1,0:T(8,128)(2,1)}, f32[8,256,256]{2,1,0:T(8,128)}, bf16[2,256,512]{2,1,0:T(8,128)(2,1)}, bf16[1...) custom-call(s32[5]{0:T(128)} %pad_add_fusion.meta, ...), custom_call_target="tpu_custom_call" | custom-call | tf_op jit(solution)/shard_map/forward/pallas_call | solution.py:1060
  274.5 92.3 %backward.1 = (bf16[128,1024]{1,0:T(8,128)(2,1)}, f32[128,1024]{1,0:T(8,128)}, f32[2,32,1536]{2,1,0:T(8,128)}, f32[32,1024]{1,0:T(8,128)}, f32[32,128]{1,0:T(8,1...) custom-call(bf16[256,1024]{1,0:T(8,128)(2,1)} %get-tuple-element.29.XG, bf16[256,1536]{1,0:T(8,128)(2,1)} %get-tuple-element.30.QKV, ...), custom_call_target="tpu_custom_call" | custom-call | tf_op jit(solution)/shard_map/backward/pallas_call | solution.py:1114
  366.8 1.4 slice_reduce_fusion
  368.2 0.8 slice_bitcast_fusion
  369.0 0.6 copy.28
  369.7 1.3 reshape.37
  370.9 0.3 copy.27
  371.2 1.1 reshape.38
  372.3 1.7 copy.36
  374.0 0.8 copy.37
  374.8 0.7 copy.38
  375.4 1.3 copy.39
  376.8 1.0 copy-done
  377.8 1.3 copy.40
  (10 shorter events, 0.1 us)
Async XLA Ops:
  366.8 7.2 %copy-start.2 = (f32[128,1024]{1,0:T(8,128)S(1)}, f32[128,1024]{1,0:T(8,128)}, u32[]{:S(2)}) copy-start(f32[128,1024]{1,0:T(8,128)} %get-tuple-element.44) | copy-start | bytes 1572868
  366.8 8.0 %copy-start.3 = (f32[32,1024]{1,0:T(8,128)S(1)}, f32[32,1024]{1,0:T(8,128)}, u32[]{:S(2)}) copy-start(f32[32,1024]{1,0:T(8,128)} %get-tuple-element.78) | copy-start | bytes 393220
  369.7 5.8 %copy-start.1 = (f32[2,256,1024]{2,1,0:T(8,128)S(1)}, f32[2,256,1024]{2,1,0:T(8,128)}, u32[]{:S(2)}) copy-start(f32[2,256,1024]{2,1,0:T(8,128)} %get-tuple-element.48) | copy-start | bytes 6291460
  375.4 2.3 copy-start

commit v2 on v1

--- a/solution.py
+++ b/solution.py
@@ -372,20 +372,28 @@
         self.dev_x = (self.gx, y, w)
         self.dev_c = (self.gc, y, w)
         self.dev_y = (g, 1 - y, w)
+        self.dev_pair = (g, y, self.w1)
         self.dev_z = lambda k: (g, y, lax.rem(w + k, 4))
 
-    def team(self, j):
-        jx, jz = lax.rem(j, 2), lax.div(j, 2)
-        tx = self.x + jx - 2 * self.x * jx
-        tz = self.wb + jz - 2 * self.wb * jz
-        return 2 * tx + tz, (2 * tx + self.c, self.y, (1 - jz) * self.w + jz * self.w1)
+    def team_places(self):
+        mine = 2 * self.x + lax.div(self.w, 2)
+        x_side = 2 * (1 - self.x) + lax.div(self.w, 2)
+        flip = 1 - 2 * lax.div(self.w, 2)
+        return mine, x_side, mine + flip, x_side + flip
 
 
 def greet(devices):
     barrier = pltpu.get_barrier_semaphore()
     for device in devices:
         pl.semaphore_signal(barrier, inc=1, device_id=device, device_id_type=MESH)
-    pl.semaphore_wait(barrier, len(devices))
+    return lambda: pl.semaphore_wait(barrier, len(devices))
+
+
+def one_hot(rows, columns):
+    same = lax.broadcasted_iota(jnp.int32, (rows, columns), 0) == lax.broadcasted_iota(
+        jnp.int32, (rows, columns), 1
+    )
+    return same.astype(F32).astype(BF)
 
 
 def dispatch_block(route_rows, expert):
@@ -399,28 +407,28 @@
     return hit.astype(F32).astype(BF)
 
 
-def place_of(meta, index):
-    place = jnp.where(index < 128, meta[3], meta[4]) * 128 + lax.rem(index, 128)
-    bound = meta[0]
+def place_of(lengths, order, index):
+    place = jnp.where(index < 128, order[0], order[1]) * 128 + lax.rem(index, 128)
+    bound = lengths[0]
     sequence = jnp.where(place >= bound, 1, 0)
     for part in (1, 2):
-        bound = bound + meta[part]
+        bound = bound + lengths[part]
         sequence = sequence + jnp.where(place >= bound, 1, 0)
     return place, sequence
 
 
 def forward_kernel(
-    meta, tok, cot, rts, wq_in, wo_in, up_in, dn_in,
-    XG, QKV, PR, MXH, WQ, WO, RT, OUTS, RESS, CGR, GU1, GD1, S2U, S2D,
-    TQ, CG, XH, NRM, UP, DN, DSP, XS, GS, MS, AA,
-    R1, R2, R3, R4, RB, PS, OWN, GP1, A1, A2, DH, SUMS,
-    GU2, GD2, CRU, CRD, ZSU, ZSD, ZRU, ZRD,
+    lengths, order, tok, cot, rts, pw, wo_in, ext, up_in, dn_in,
+    XG, QKV, PR, MXH, W0, W1, W2, WO, RT, OUTS, RESS, CGR, P1U, P1D, Z1U, Z1D, S2U, S2D,
+    WS0, WS1, WS2, CG, XH, NRM, UP, DN, DSP, XS, GS, MS, AA,
+    R1, R2, R3, R4, RB, PS, OWN, RES, GP1, A1, A2, DH, SUMS,
+    GU, GD, CRU, CRD, P2U, P2D, ZSU, ZSD, ZRU, ZRD,
     send, recv, local,
 ):
     p = Place()
     g, y, w, x = p.g, p.y, p.w, p.x
     cp = Copies(send, recv)
-    greet([p.dev_x, p.dev_c, p.dev_y, p.dev_z(1), p.dev_z(2), p.dev_z(3), p.team(3)[1]])
+    all_in = greet([p.dev_x, p.dev_c, p.dev_y, p.dev_z(1), p.dev_z(2), p.dev_z(3)])
     nlocal = [0]
 
     def here(src, dst):
@@ -436,31 +444,39 @@
         for item in items:
             item.wait()
 
-    mine = pl.ds(y * 128, 128)
-    row = pl.ds(pl.multiple_of(g * 256 + y * 128 + w * 32, 32), 32)
+    W, WS = (W0, W1, W2), (WS0, WS1, WS2)
+    for ch in range(3):
+        for t in range(4):
+            for plane in (0, 1):
+                first = ch * 1024 + t * 256 + plane * 128
+                WS[ch][plane, :, t * 128 : (t + 1) * 128] = pw[:, first : first + 128]
+    extra_rows = jnp.concatenate([ext[...], jnp.zeros((EXTRA - 8, EXTRA), F32)], axis=0).astype(BF)
+    extra_cols = dot(one_hot(32, EXTRA), extra_rows, NT).astype(BF)
+    WS0[0, :, 512:] = extra_cols
+    WS0[1, :, 512:] = extra_cols
+    RT[y] = jnp.broadcast_to(rts[...].astype(F32), (8, 128))
+    mine = pl.ds(pl.multiple_of(y * 128, 128), 128)
+    XG[mine, :] = tok[...]
+    CG[mine, :] = cot[...]
+
+    def row(plane):
+        return pl.ds(pl.multiple_of(g * 256 + plane * 128 + w * 32, 32), 32)
+
+    for ch in range(3):
+        W[ch][row(y), :] = WS[ch][y]
     row_o = pl.ds(pl.multiple_of(g * 128 + w * 32, 32), 32)
-    row_t = pl.ds(pl.multiple_of(w * 32, 32), 32)
-    zq = []
-    zo = []
-    for k in (1, 3, 2):
-        zq += go(
-            cp.new(wq_in.at[y], WQ.at[row, :], p.dev_z(k)),
-            cp.new(wq_in.at[1 - y], TQ.at[row_t, :], p.dev_z(k)),
-        )
-    own = go(
-        here(wq_in.at[y], WQ.at[row, :]),
-        here(wq_in.at[1 - y], TQ.at[row_t, :]),
-        here(wo_in, WO.at[y, row_o, :]),
-        here(tok, XG.at[mine, :]),
-        here(cot, CG.at[mine, :]),
-        here(rts, RT.at[y]),
-    )
-    ty = go(
-        cp.new(tok, XG.at[mine, :], p.dev_y),
-        cp.new(rts, RT.at[y], p.dev_y),
-    )
-    for k in (1, 3, 2):
-        zo += go(cp.new(wo_in, WO.at[y, row_o, :], p.dev_z(k)))
+    WO[y, row_o, :] = wo_in[...]
+    all_in()
+
+    def z_rows(ch, plane):
+        return sum(
+            (go(cp.new(W[ch].at[row(plane), :], W[ch].at[row(plane), :], p.dev_z(k))) for k in (2, 1, 3)), ()
+        )
+
+    yw = [go(cp.new(WS[ch].at[1 - y], W[ch].at[row(y), :], p.dev_y)) for ch in range(3)]
+    zo = sum((go(cp.new(wo_in, WO.at[y, row_o, :], p.dev_z(k))) for k in (2, 1, 3)), ())
+    zw = [z_rows(0, y), (), ()]
+    ty = go(cp.new(RT.at[y], RT.at[y], p.dev_y), cp.new(tok, XG.at[mine, :], p.dev_y))
 
     def dq(q):
         return pl.ds(pl.multiple_of(q * 256, 256), 256)
@@ -488,14 +504,14 @@
 
     def e_z(s):
         return go(
-            cp.new(up_in.at[s, :, half], UP.at[s, 1, dq(g), :], p.dev_z(2)),
-            cp.new(dn_in.at[s, half, :], DN.at[s, 1, :, dq(g)], p.dev_z(2)),
+            cp.new(up_in.at[s, :, half], UP.at[s, 1, dq(g), :], p.dev_pair),
+            cp.new(dn_in.at[s, half, :], DN.at[s, 1, :, dq(g)], p.dev_pair),
         )
 
     def e_relay(s):
         return go(
-            cp.new(UP.at[s, 0, dq(p.gx), :], UP.at[s, 1, dq(p.gx), :], p.dev_z(2)),
-            cp.new(DN.at[s, 0, :, dq(p.gx)], DN.at[s, 1, :, dq(p.gx)], p.dev_z(2)),
+            cp.new(UP.at[s, 0, dq(p.gx), :], UP.at[s, 1, dq(p.gx), :], p.dev_pair),
+            cp.new(DN.at[s, 0, :, dq(p.gx)], DN.at[s, 1, :, dq(p.gx)], p.dev_pair),
         )
 
     def e_core(s, q, which):
@@ -504,13 +520,15 @@
             cp.new(DN.at[s, q, :, dq(which)], DN.at[s, q, :, dq(which)], p.dev_c),
         )
 
-    e1 = [e_first(0)]
+    wait(*yw[0])
+    zw[0] += z_rows(0, 1 - y)
+    for ch in (1, 2):
+        wait(*yw[ch])
+        zw[ch] = z_rows(ch, y) + z_rows(ch, 1 - y)
     el = e_local(0) + e_local(1)
-    ec0 = [e_core0(0), e_core0(1)]
-
-    wait(*own)
+    ec0 = [e_core0(0)]
+
     wait(*ty)
-    cy = go(cp.new(cot, CG.at[mine, :], p.dev_y))
     values = XG[...].astype(F32)
     centred = values - jnp.mean(values, axis=1, keepdims=True)
     inverse = lax.rsqrt(jnp.mean(centred * centred, axis=1, keepdims=True) + 1e-05)
@@ -519,53 +537,56 @@
         DSP[b] = dispatch_block(RT[b], y)
         XS[b * CAP : (b + 1) * CAP, :] = dot(DSP[b], XG[b * 128 : (b + 1) * 128, :])
 
-    wait(*zq)
-    yq = go(cp.new(TQ, WQ.at[pl.ds(pl.multiple_of(g * 256 + y * 128, 128), 128), :], p.dev_y))
-    wait(*e1[0])
-    ez = [e_z(0)]
-    er = [e_relay(0)]
-    ec = [e_core(0, 0, p.gx)]
+    def quarter(d):
+        return pl.ds(pl.multiple_of(d * 128, 128), 128)
+
+    def wo_copy(plane, d, device):
+        return cp.new(WO.at[plane, quarter(d), :], WO.at[plane, quarter(d), :], device)
+
+    def w_copy(ch, d, device):
+        return cp.new(W[ch].at[dq(d), :], W[ch].at[dq(d), :], device)
+
+    xw, fw = [None] * 3, [None] * 3
     wait(*zo)
-    block_y = pl.ds(pl.multiple_of(g * 128, 128), 128)
-    yo = go(cp.new(WO.at[y, block_y, :], WO.at[y, block_y, :], p.dev_y))
-    wait(*yq)
-    xq = go(
-        cp.new(WQ.at[dq(g), :], WQ.at[dq(g), :], p.dev_x),
-        cp.new(WQ.at[dq(g), :], WQ.at[dq(g), :], p.dev_c),
-    )
-    wait(*yo)
-    xo = go(
-        cp.new(WO.at[:, block_y, :], WO.at[:, block_y, :], p.dev_x),
-        cp.new(WO.at[:, block_y, :], WO.at[:, block_y, :], p.dev_c),
-    )
-    e1.append(e_first(1))
-    wait(*xq)
-    fq = go(cp.new(WQ.at[dq(p.gx), :], WQ.at[dq(p.gx), :], p.dev_c))
-    wait(*cy)
-    for b in (0, 1):
-        GS[b * CAP : (b + 1) * CAP, :] = dot(DSP[b], CG[b * 128 : (b + 1) * 128, :]).astype(BF)
-    wait(*fq)
-
-    pick = (
-        lax.broadcasted_iota(jnp.int32, (8, EXTRA), 0) == lax.broadcasted_iota(jnp.int32, (8, EXTRA), 1)
-    ).astype(F32).astype(BF)
-    extra = dot(pick, WQ[:, 1536:], NT)
+    xo = go(wo_copy(y, g, p.dev_x))
+    wait(*zw[0])
+    xw[0] = go(w_copy(0, g, p.dev_x), w_copy(0, g, p.dev_c))
+    wait(*xo)
+    yo = go(wo_copy(y, g, p.dev_y), wo_copy(y, p.gx, p.dev_y))
+    co = go(wo_copy(y, g, p.dev_c), wo_copy(y, p.gx, p.dev_c))
+    wait(*zw[1])
+    xw[1] = go(w_copy(1, g, p.dev_x), w_copy(1, g, p.dev_c))
+    wait(*zw[2])
+    xw[2] = go(w_copy(2, g, p.dev_x), w_copy(2, g, p.dev_c))
+    ez = [e_z(0), e_z(1)]
+    e1 = [e_first(0), e_first(1)]
+    ec0.append(e_core0(1))
+    cy = go(cp.new(cot, CG.at[mine, :], p.dev_y))
+    wait(*xw[0])
+    fw[0] = go(w_copy(0, p.gx, p.dev_c))
+    wait(*fw[0])
+    extra = dot(one_hot(8, EXTRA), W0[:, 512:], NT)
     gain = extra[0:1, :]
     centroid = jnp.where(y == 0, extra[1:2, :], extra[2:3, :])
     NRM[...] = (XH[...] * gain).astype(BF)
 
-    def project(t, carry):
-        cols = pl.ds(pl.multiple_of(t * 512, 512), 512)
-        QKV[:, cols] = dot(NRM[...], WQ[:, cols]).astype(BF)
-        return carry
-
-    lax.fori_loop(0, 3, project, 0)
-    wait(*xo)
-    far = pl.ds(pl.multiple_of(p.gx * 128, 128), 128)
-    fo = go(cp.new(WO.at[:, far, :], WO.at[:, far, :], p.dev_c))
-
-    place_q, seq_q = place_of(meta, lax.broadcasted_iota(jnp.int32, (256, 256), 0))
-    place_k, seq_k = place_of(meta, lax.broadcasted_iota(jnp.int32, (256, 256), 1))
+    def project(ch):
+        QKV[:, ch * 512 : (ch + 1) * 512] = dot(NRM[...], W[ch][:, :512]).astype(BF)
+
+    project(0)
+    wait(*xw[1])
+    fw[1] = go(w_copy(1, p.gx, p.dev_c))
+    wait(*fw[1])
+    project(1)
+    wait(*yo)
+    co += go(wo_copy(1 - y, g, p.dev_c), wo_copy(1 - y, p.gx, p.dev_c))
+    wait(*xw[2])
+    fw[2] = go(w_copy(2, p.gx, p.dev_c))
+    wait(*fw[2])
+    project(2)
+
+    place_q, seq_q = place_of(lengths, order, lax.broadcasted_iota(jnp.int32, (256, 256), 0))
+    place_k, seq_k = place_of(lengths, order, lax.broadcasted_iota(jnp.int32, (256, 256), 1))
     allowed = (seq_q == seq_k) & (place_k <= place_q)
     low_half = lax.broadcasted_iota(jnp.int32, (256, 128), 1) < 64
     mixed_first = cp.block(4)
@@ -598,8 +619,14 @@
         for b in (0, 1):
             MS[yy, b * CAP : (b + 1) * CAP, :] = dot(DSP[b], MXH[yy, b * 128 : (b + 1) * 128, :]).astype(BF)
 
+    wait(*e1[0])
+    er = [e_relay(0)]
+    ec = [e_core(0, 0, p.gx)]
     mixed_pick(y)
-    wait(*fo)
+    wait(*cy)
+    for b in (0, 1):
+        GS[b * CAP : (b + 1) * CAP, :] = dot(DSP[b], CG[b * 128 : (b + 1) * 128, :]).astype(BF)
+    wait(*co)
     AA[...] = XS[...] + dot(MS[y], WO[y])
     lax.fori_loop(0, 4, lambda t, carry: (mixed_copy(t).wait(), carry)[1], 0)
     mixed_pick(1 - y)
@@ -607,40 +634,87 @@
     gate = jax.nn.sigmoid(jnp.sum(AA[...] * centroid, axis=1, keepdims=True))
 
     wait(*el)
-    me = pl.ds(pl.multiple_of(p.team(0)[0] * 160, 160), 160)
-
-    def spread(first, R):
-        def one(j):
-            device = p.team(j)[1]
-            return cp.at(first + j - 1, R.at[me, :], R.at[me, :], device)
-
-        return one
+    at_me, at_x, at_z, at_d = p.team_places()
+
+    def rows_of(place):
+        return pl.ds(pl.multiple_of(place * 160, 32), 160)
+
+    def part(i, place=0):
+        return pl.ds(pl.multiple_of(place * 160 + i * 32, 32), 32)
 
     def each(fn):
-        def body(j, carry):
-            fn(j)
+        def body(i, carry):
+            fn(i)
             return carry
 
-        lax.fori_loop(1, 4, body, 0)
-
-    def reduce_copy(first, k, b):
-        def one(j):
-            device = p.team(j)[1]
-            return cp.at(first + j - 1, PS.at[k, j - 1], RB.at[b, j - 1], device)
-
-        return one
-
-    firsts = [cp.block(3) for _ in range(8)]
-    g1, g2, g3, g4 = (spread(f, R) for f, R in zip(firsts[:4], (R1, R2, R3, R4)))
-    r1, r3, r2, r4 = (reduce_copy(f, k, b) for f, k, b in zip(firsts[4:], (0, 1, 2, 0), (0, 1, 2, 3)))
-
-    def rows_of(j):
-        return pl.ds(pl.multiple_of(p.team(j)[0] * 160, 160), 160)
-
-    R1[me, :] = AA[...].astype(BF)
-    each(lambda j: g1(j).start())
-    R3[me, :] = (gate * GS[...].astype(F32)).astype(BF)
-    each(lambda j: g3(j).start())
+        lax.fori_loop(0, 5, body, 0)
+
+    class Spread:
+        def __init__(self, R):
+            self.R = R
+            self.zi, self.xi, self.fi = cp.block(5), cp.block(5), cp.block(5)
+
+        def same(self, first, i, place, device):
+            view = self.R.at[part(i, place), :]
+            return cp.at(first + i, view, view, device)
+
+        def z(self, i):
+            return self.same(self.zi, i, at_me, p.dev_z(2))
+
+        def x(self, i):
+            return self.same(self.xi, i, at_me, p.dev_x)
+
+        def forward(self, i):
+            return self.same(self.fi, i, at_z, p.dev_x)
+
+        def start_part(self, i):
+            self.z(i).start()
+            self.x(i).start()
+
+        def relay_part(self, i):
+            self.z(i).wait()
+            self.forward(i).start()
+
+    class Reduce:
+        def __init__(self, staging, landing):
+            self.put, self.got = PS.at[staging], RB.at[landing]
+            self.xi, self.di, self.zi = cp.block(1), cp.block(5), cp.block(5)
+
+        def x(self):
+            return cp.at(self.xi, self.put.at[0], self.got.at[0], p.dev_x)
+
+        def d(self, i):
+            return cp.at(self.di + i, self.put.at[1, part(i), :], self.got.at[1, part(i), :], p.dev_x)
+
+        def z(self, i):
+            return cp.at(self.zi + i, self.put.at[2, part(i), :], self.got.at[2, part(i), :], p.dev_z(2))
+
+        def start_x(self):
+            each(lambda i: self.d(i).start())
+            self.x().start()
+
+        def relay_part(self, i, own_z):
+            self.d(i).wait()
+            self.put[2, part(i), :] = (own_z[part(i), :] + self.got[1, part(i), :].astype(F32)).astype(BF)
+            self.z(i).start()
+
+        def result_part(self, i, own):
+            self.z(i).wait()
+            return (
+                own[part(i), :]
+                + self.got[0, part(i), :].astype(F32)
+                + self.got[2, part(i), :].astype(F32)
+            )
+
+    g1, g2, g3, g4 = Spread(R1), Spread(R2), Spread(R3), Spread(R4)
+    r1, r2, r3, r4 = Reduce(0, 0), Reduce(1, 1), Reduce(0, 2), Reduce(0, 3)
+    mine_r = rows_of(at_me)
+
+    R1[mine_r, :] = AA[...].astype(BF)
+    each(lambda i: g1.z(i).start())
+    each(lambda i: g1.x(i).start())
+    R3[mine_r, :] = (gate * GS[...].astype(F32)).astype(BF)
+    each(lambda i: g3.z(i).start())
 
     wait(*ec0[0])
     wait(*ec[0])
@@ -648,18 +722,14 @@
     ec1 = e_core(0, 1, g)
     wait(*er[0])
     ec2 = e_core(0, 1, p.gx)
-    wait(*e1[1])
-    ez.append(e_z(1))
-    er.append(e_relay(1))
-    ec.append(e_core(1, 0, p.gx))
     wait(*ec1)
     wait(*ec2)
 
     def cols_of(q):
         return slice(q * 512, (q + 1) * 512)
 
-    def first_forward(j):
-        at = rows_of(j)
+    def first_forward(place):
+        at = rows_of(place)
         total = None
         for q in (0, 1):
             active, slope = gelu_both(dot(R1[at, :], UP[0, q]))
@@ -669,20 +739,29 @@
             total = term if total is None else total + term
         return total
 
-    OWN[0] = first_forward(0)
-
-    def step_one(j):
-        g1(j).wait()
-        PS[0, j - 1] = first_forward(j).astype(BF)
-        r1(j).start()
-
-    each(step_one)
-    each(lambda j: r1(j).wait())
-    branch_one = OWN[0] + RB[0, 0].astype(F32) + RB[0, 1].astype(F32) + RB[0, 2].astype(F32)
-    SUMS[0] = branch_one
-    R2[me, :] = (AA[...].astype(BF).astype(F32) + branch_one).astype(BF)
-    each(lambda j: g2(j).start())
-    each(lambda j: g3(j).wait())
+    OWN[0] = first_forward(at_me)
+    each(g1.relay_part)
+    each(lambda i: g1.x(i).wait())
+    PS[0, 0] = first_forward(at_x).astype(BF)
+    OWN[3] = first_forward(at_z)
+    each(lambda i: g1.forward(i).wait())
+    PS[0, 1] = first_forward(at_d).astype(BF)
+    r1.start_x()
+    wait(*e1[1])
+    er.append(e_relay(1))
+    ec.append(e_core(1, 0, p.gx))
+    each(lambda i: r1.relay_part(i, OWN.at[3]))
+    each(lambda i: g3.x(i).start())
+    r1.x().wait()
+
+    def middle_part(i):
+        branch = r1.result_part(i, OWN.at[0])
+        SUMS[0, part(i), :] = branch
+        R2[part(i, at_me), :] = (AA[part(i), :].astype(BF).astype(F32) + branch).astype(BF)
+        g2.start_part(i)
+
+    each(middle_part)
+    each(g3.relay_part)
 
     wait(*ec0[1])
     wait(*ec[1])
@@ -693,9 +772,9 @@
     wait(*ec1)
     wait(*ec2)
 
-    def second_both(j):
-        at = rows_of(j)
-        total, total_grad = None, None
+    def second_grad(place):
+        at = rows_of(place)
+        total_grad = None
         for q in (0, 1):
             active, slope = gelu_both(dot(R2[at, :], UP[1, q]))
             A2[at, cols_of(q)] = active.astype(BF)
@@ -703,22 +782,28 @@
             DH[at, cols_of(q)] = grad
             term = dot(grad, UP[1, q], NT)
             total_grad = term if total_grad is None else total_grad + term
-        for q in (0, 1):
-            term = dot(A2[at, cols_of(q)], DN[1, q])
-            total = term if total is None else total + term
-        return total, total_grad
-
-    OWN[1], OWN[2] = second_both(0)
-
-    def step_two(j):
-        g2(j).wait()
-        total, total_grad = second_both(j)
-        PS[1, j - 1] = total_grad.astype(BF)
-        r3(j).start()
-        PS[2, j - 1] = total.astype(BF)
-        r2(j).start()
-
-    each(step_two)
+        return total_grad
+
+    def second_forward(place):
+        at = rows_of(place)
+        return dot(A2[at, :512], DN[1, 0]) + dot(A2[at, 512:], DN[1, 1])
+
+    OWN[2] = second_grad(at_me)
+    OWN[1] = second_forward(at_me)
+    each(g2.relay_part)
+    each(lambda i: g2.x(i).wait())
+    each(lambda i: g3.x(i).wait())
+    PS[0, 0] = second_grad(at_x).astype(BF)
+    OWN[3] = second_grad(at_z)
+    each(lambda i: g2.forward(i).wait())
+    each(lambda i: g3.forward(i).wait())
+    PS[0, 1] = second_grad(at_d).astype(BF)
+    r3.start_x()
+    PS[1, 1] = second_forward(at_d).astype(BF)
+    PS[1, 0] = second_forward(at_x).astype(BF)
+    OWN[4] = second_forward(at_z)
+    each(lambda i: r3.relay_part(i, OWN.at[3]))
+    r2.start_x()
 
     def weight_grads(A, R, RG, GU, GD):
         def one(q, d):
@@ -736,42 +821,50 @@
 
         return body
 
-    body2 = weight_grads(A2, R2, R3, GU2, GD2)
+    def to_core(n):
+        out = ()
+        for k, theirs in enumerate((p.gc, p.gd)):
+            out += go(
+                cp.new(GU.at[:, theirs], CRU.at[n, :, k], p.dev_c),
+                cp.new(GD.at[:, theirs], CRD.at[n, :, k], p.dev_c),
+            )
+        return out
+
+    def add_core(n, own_u, own_d, far_u, far_d):
+        for k, d in enumerate((g, p.gx)):
+            far_u[k] = (GU[1, d].astype(F32) + CRU[n, 1, k].astype(F32)).astype(BF)
+            far_d[k] = (GD[1, d].astype(F32) + CRD[n, 1, k].astype(F32)).astype(BF)
+            own_u[k] = (GU[0, d].astype(F32) + CRU[n, 0, k].astype(F32)).astype(BF)
+            own_d[k] = (GD[0, d].astype(F32) + CRD[n, 0, k].astype(F32)).astype(BF)
+
+    body2 = weight_grads(A2, R2, R3, GU, GD)
     lax.fori_loop(0, 4, body2, 0)
-    f0 = []
-    for k, (theirs, mine_d) in enumerate(((p.gc, 0), (p.gd, 1))):
-        f0 += go(
-            cp.new(GU2.at[:, theirs], CRU.at[:, k], p.dev_c),
-            cp.new(GD2.at[:, theirs], CRD.at[:, k], p.dev_c),
-        )
+    f0 = to_core(0)
     lax.fori_loop(4, 8, body2, 0)
 
-    each(lambda j: r3(j).wait())
-    middle_grad = OWN[2] + RB[1, 0].astype(F32) + RB[1, 1].astype(F32) + RB[1, 2].astype(F32)
-    SUMS[1] = middle_grad
-    R4[me, :] = (R3[me, :].astype(F32) + middle_grad).astype(BF)
-    each(lambda j: g4(j).start())
+    r3.x().wait()
+
+    def middle_grad_part(i):
+        total = r3.result_part(i, OWN.at[2])
+        SUMS[1, part(i), :] = total
+        R4[part(i, at_me), :] = (R3[part(i, at_me), :].astype(F32) + total).astype(BF)
+        g4.start_part(i)
+
+    each(middle_grad_part)
     wait(*f0)
+    add_core(0, P2U, P2D, ZSU, ZSD)
     f1 = []
-    for k, d in enumerate((g, p.gx)):
-        ZSU[k] = (GU2[1, d].astype(F32) + CRU[1, k].astype(F32)).astype(BF)
-        ZSD[k] = (GD2[1, d].astype(F32) + CRD[1, k].astype(F32)).astype(BF)
+    for k in (0, 1):
         f1 += go(
-            cp.new(ZSU.at[k], ZRU.at[k], p.dev_z(2)),
-            cp.new(ZSD.at[k], ZRD.at[k], p.dev_z(2)),
-        )
-
-    each(lambda j: r2(j).wait())
-    branch_two = OWN[1] + RB[2, 0].astype(F32) + RB[2, 1].astype(F32) + RB[2, 2].astype(F32)
-    returned = (SUMS[0] + branch_two).astype(BF).astype(F32)
-    upstream = GS[...].astype(F32)
-    OUTS[...] = (AA[...] + gate * returned).astype(BF)
-    score_grad = jnp.sum(upstream * returned, axis=1, keepdims=True) * gate * (1.0 - gate)
-    CGR[...] = jnp.broadcast_to(jnp.sum(score_grad * AA[...], axis=0, keepdims=True), CGR.shape)
-    OWN[1] = upstream + score_grad * centroid
-
-    def first_backward(j):
-        at = rows_of(j)
+            cp.new(ZSU.at[k], ZRU.at[k], p.dev_pair),
+            cp.new(ZSD.at[k], ZRD.at[k], p.dev_pair),
+        )
+
+    each(lambda i: r2.relay_part(i, OWN.at[4]))
+    r2.x().wait()
+
+    def first_backward(place):
+        at = rows_of(place)
         total = None
         for q in (0, 1):
             grad = (GP1[at, cols_of(q)] * dot(R4[at, :], DN[0, q], NT)).astype(BF)
@@ -780,40 +873,66 @@
             total = term if total is None else total + term
         return total
 
-    OWN[0] = first_backward(0)
-
-    def step_three(j):
-        g4(j).wait()
-        PS[0, j - 1] = first_backward(j).astype(BF)
-        r4(j).start()
-
-    each(step_three)
-    lax.fori_loop(0, 8, weight_grads(A1, R1, R4, GU1, GD1), 0)
-    each(lambda j: r4(j).wait())
-    arrived = (
-        OWN[0] + RB[3, 0].astype(F32) + RB[3, 1].astype(F32) + RB[3, 2].astype(F32) + SUMS[1]
-    ).astype(BF)
-    RESS[...] = (OWN[1] + arrived.astype(F32)).astype(BF)
-
+    OWN[0] = first_backward(at_me)
+    each(g4.relay_part)
+    each(lambda i: g4.x(i).wait())
+    PS[0, 0] = first_backward(at_x).astype(BF)
+    OWN[3] = first_backward(at_z)
+    each(lambda i: g4.forward(i).wait())
+    PS[0, 1] = first_backward(at_d).astype(BF)
+    r4.start_x()
+
+    def output_part(i):
+        branch_two = r2.result_part(i, OWN.at[1])
+        returned = (SUMS[0, part(i), :] + branch_two).astype(BF).astype(F32)
+        upstream = GS[part(i), :].astype(F32)
+        after = AA[part(i), :]
+        gate_part = jax.nn.sigmoid(jnp.sum(after * centroid, axis=1, keepdims=True))
+        OUTS[part(i), :] = (after + gate_part * returned).astype(BF)
+        score_grad = jnp.sum(upstream * returned, axis=1, keepdims=True) * gate_part * (1.0 - gate_part)
+        RES[part(i), :] = upstream + score_grad * centroid
+        CGR[...] += jnp.broadcast_to(jnp.sum(score_grad * after, axis=0, keepdims=True), CGR.shape)
+
+    CGR[...] = jnp.zeros_like(CGR)
+
+    each(lambda i: r4.relay_part(i, OWN.at[3]))
+    each(output_part)
+    body1 = weight_grads(A1, R1, R4, GU, GD)
+    lax.fori_loop(0, 4, body1, 0)
+    f0 = to_core(1)
+    lax.fori_loop(4, 8, body1, 0)
+    r4.x().wait()
+
+    def residual_part(i):
+        arrived = (r4.result_part(i, OWN.at[0]) + SUMS[1, part(i), :]).astype(BF)
+        RESS[part(i), :] = (RES[part(i), :] + arrived.astype(F32)).astype(BF)
+
+    each(residual_part)
+    wait(*f0)
+    add_core(1, P1U, P1D, Z1U, Z1D)
     wait(*f1)
-    for k, d in enumerate((g, p.gx)):
-        S2U[k] = GU2[0, d].astype(F32) + CRU[0, k].astype(F32) + ZRU[k].astype(F32)
-        S2D[k] = GD2[0, d].astype(F32) + CRD[0, k].astype(F32) + ZRD[k].astype(F32)
+    for k in (0, 1):
+        S2U[k] = P2U[k].astype(F32) + ZRU[k].astype(F32)
+        S2D[k] = P2D[k].astype(F32) + ZRD[k].astype(F32)
 
 
 def backward_kernel(
-    XG, QKV, PR, MXH, WQ, WO, RT, OUTS, RESS, CGR, GU, GD, S2U, S2D,
+    XG, QKV, PR, MXH, W0, W1, W2, WO, RT, OUTS, RESS, CGR, P1U, P1D, Z1U, Z1D, S2U, S2D,
     out, tgrad, pgrad, ograd, egrad, ugrad, dgrad,
     RP, OP, RL, XH, NRM, MG, DQ, NG, NGS, NGR,
-    CRU, CRD, ZSU, ZSD, ZRU, ZRD, XSU, XSD, XRU, XRD,
+    ZRU, ZRD, XSU, XSD, XRU, XRD,
     PW, PC, PXS, PXR, PYS, PYR, PK, PZR,
-    OW, OC, OXS, OXR, OK, OZR,
+    OW, OC, OXS, OXR, OK, OZR, TE,
     send, recv,
 ):
     p = Place()
     g, y, w, x = p.g, p.y, p.w, p.x
     cp = Copies(send, recv)
-    greet([p.dev_x, p.dev_c, p.dev_y, p.dev_z(1), p.dev_z(2), p.dev_z(3)])
+    W = (W0, W1, W2)
+    all_in = greet([p.dev_x, p.dev_c, p.dev_y, p.dev_z(1), p.dev_z(2), p.dev_z(3)])
+    XSU[1] = S2U[1].astype(BF)
+    XSD[1] = S2D[1].astype(BF)
+    all_in()
 
     def go(*items):
         for item in items:
@@ -829,14 +948,12 @@
     ry = go(cp.new(RESS, RP, p.dev_y))
     oy = go(cp.new(OUTS.at[peer_slots, :], OP, p.dev_y))
 
-    f0 = []
-    for k, theirs in enumerate((p.gc, p.gd)):
-        f0 += go(
-            cp.new(GU.at[:, theirs], CRU.at[:, k], p.dev_c),
-            cp.new(GD.at[:, theirs], CRD.at[:, k], p.dev_c),
-        )
-    XSU[1] = S2U[1].astype(BF)
-    XSD[1] = S2D[1].astype(BF)
+    f1 = []
+    for k in (1, 0):
+        f1 += go(
+            cp.new(Z1U.at[k], ZRU.at[k], p.dev_pair),
+            cp.new(Z1D.at[k], ZRD.at[k], p.dev_pair),
+        )
     f2 = {1: go(cp.new(XSU.at[1], XRU.at[1], p.dev_x), cp.new(XSD.at[1], XRD.at[1], p.dev_x))}
 
     half = pl.ds(pl.multiple_of(x * 512, 512), 512)
@@ -848,21 +965,9 @@
     centred = values - jnp.mean(values, axis=1, keepdims=True)
     inverse = lax.rsqrt(jnp.mean(centred * centred, axis=1, keepdims=True) + 1e-05)
     XH[...] = centred * inverse
-    pick = (
-        lax.broadcasted_iota(jnp.int32, (8, EXTRA), 0) == lax.broadcasted_iota(jnp.int32, (8, EXTRA), 1)
-    ).astype(F32).astype(BF)
-    gain = dot(pick, WQ[:, 1536:], NT)[0:1, :]
+    pick = one_hot(8, EXTRA)
+    gain = dot(pick, W0[:, 512:], NT)[0:1, :]
     NRM[...] = (XH[...] * gain).astype(BF)
-
-    wait(*f0)
-    f1 = []
-    for k, d in enumerate((g, p.gx)):
-        ZSU[k] = (GU[1, d].astype(F32) + CRU[1, k].astype(F32)).astype(BF)
-        ZSD[k] = (GD[1, d].astype(F32) + CRD[1, k].astype(F32)).astype(BF)
-        f1 += go(
-            cp.new(ZSU.at[k], ZRU.at[k], p.dev_z(2)),
-            cp.new(ZSD.at[k], ZRD.at[k], p.dev_z(2)),
-        )
 
     wait(*ry)
     for b in (0, 1):
@@ -913,7 +1018,9 @@
 
     lax.fori_loop(0, 4, heads, 0)
 
-    NG[...] = dot(DQ[...], WQ[:, :1536], NT)
+    NG[...] = (
+        dot(DQ[:, :512], W0[:, :512], NT) + dot(DQ[:, 512:1024], W1[...], NT) + dot(DQ[:, 1024:], W2[...], NT)
+    )
     NGS[...] = NG[pl.ds(pl.multiple_of((1 - y) * 128, 128), 128), :].astype(BF)
     ny = go(cp.new(NGS, NGR, p.dev_y))
     gain_row = jnp.sum(NG[...] * XH[...], axis=0, keepdims=True)
@@ -993,10 +1100,10 @@
         pz += go(cp.new(PYR.at[row32(lax.rem(w + k, 4)), :], PZR.at[k - 1, 1], p.dev_z(k)))
 
     wait(*f1)
-    ugrad[0, :, half] = GU[0, g].astype(F32) + CRU[0, 0].astype(F32) + ZRU[0].astype(F32)
-    dgrad[0, half, :] = GD[0, g].astype(F32) + CRD[0, 0].astype(F32) + ZRD[0].astype(F32)
-    XSU[0] = (GU[0, p.gx].astype(F32) + CRU[0, 1].astype(F32) + ZRU[1].astype(F32)).astype(BF)
-    XSD[0] = (GD[0, p.gx].astype(F32) + CRD[0, 1].astype(F32) + ZRD[1].astype(F32)).astype(BF)
+    ugrad[0, :, half] = P1U[0].astype(F32) + ZRU[0].astype(F32)
+    dgrad[0, half, :] = P1D[0].astype(F32) + ZRD[0].astype(F32)
+    XSU[0] = (P1U[1].astype(F32) + ZRU[1].astype(F32)).astype(BF)
+    XSD[0] = (P1D[1].astype(F32) + ZRD[1].astype(F32)).astype(BF)
     f2[0] = go(cp.new(XSU.at[0], XRU.at[0], p.dev_x), cp.new(XSD.at[0], XRD.at[0], p.dev_x))
     for s in (1, 0):
         wait(*f2[s])
@@ -1017,9 +1124,14 @@
             + PZR[1, i].astype(F32)
             + PZR[2, i].astype(F32)
         )
-    pgrad[y] = sums[0][:, :1536]
-    pgrad[1 - y] = sums[1][:, :1536]
-    egrad[...] = sums[0][:, 1536:] + sums[1][:, 1536:]
+    for plane in (0, 1):
+        kept = jnp.where(y == plane, sums[0], sums[1])
+        for ch in range(3):
+            for t in range(4):
+                first = ch * 1024 + t * 256 + plane * 128
+                pgrad[:, first : first + 128] = kept[:, ch * 512 + t * 128 : ch * 512 + (t + 1) * 128]
+    TE[0:32, :] = sums[0][:, 1536:] + sums[1][:, 1536:]
+    egrad[...] = TE[...].T[0:8, :]
 
 
 def vmem(shape, dtype=BF):
@@ -1034,26 +1146,26 @@
     in_any = pl.BlockSpec(memory_space=pl.ANY)
     in_smem = pl.BlockSpec(memory_space=pltpu.SMEM)
     shape = jax.ShapeDtypeStruct
-    extra = jnp.concatenate(
-        [norm_gain[:, None], centroids.T, jnp.zeros((32, EXTRA - 3), BF)], axis=1
-    )
-    by_plane = project_weight.reshape(32, 3, 4, 2, 128).transpose(3, 0, 1, 2, 4).reshape(2, 32, 1536)
-    wq = jnp.concatenate([by_plane, jnp.broadcast_to(extra[None], (2, 32, EXTRA))], axis=2)
-    meta = jnp.concatenate([sequence_lengths[0], block_order[0]])
-    rts = jnp.broadcast_to(routes[0, :, 0].astype(F32)[None, :], (8, 128))
+    ext = jnp.pad(
+        jnp.concatenate([norm_gain[None], centroids], axis=0).astype(F32), ((0, 5), (0, EXTRA - 32))
+    )
     mid_shapes = [
         ((256, 1024), BF),
         ((256, 1536), BF),
         ((8, 256, 256), F32),
         ((2, 256, 512), BF),
-        ((1024, 1536 + EXTRA), BF),
+        ((1024, 512 + EXTRA), BF),
+        ((1024, 512), BF),
+        ((1024, 512), BF),
         ((2, 512, 1024), BF),
         ((2, 8, 128), F32),
         ((160, 1024), BF),
         ((160, 1024), BF),
         ((8, 1024), F32),
-        ((2, 4, 256, 512), BF),
-        ((2, 4, 512, 256), BF),
+        ((2, 256, 512), BF),
+        ((2, 512, 256), BF),
+        ((2, 256, 512), BF),
+        ((2, 512, 256), BF),
         ((2, 256, 512), F32),
         ((2, 512, 256), F32),
     ]
@@ -1061,10 +1173,12 @@
         forward_kernel,
         name="forward",
         out_shape=[shape(*s) for s in mid_shapes],
-        in_specs=[in_smem] + [in_vmem] * 5 + [in_any] * 2,
+        in_specs=[in_smem] * 2 + [in_vmem] * 6 + [in_any] * 2,
         out_specs=[in_vmem] * len(mid_shapes),
         scratch_shapes=[
-            vmem((128, 1536 + EXTRA)),
+            vmem((2, 32, 512 + EXTRA)),
+            vmem((2, 32, 512)),
+            vmem((2, 32, 512)),
             vmem((256, 1024)),
             vmem((256, 1024), F32),
             vmem((256, 1024)),
@@ -1079,8 +1193,9 @@
         + [vmem((640, 1024))] * 4
         + [
             vmem((4, 3, 160, 1024)),
-            vmem((3, 3, 160, 1024)),
-            vmem((3, 160, 1024), F32),
+            vmem((2, 3, 160, 1024)),
+            vmem((5, 160, 1024), F32),
+            vmem((160, 1024), F32),
             vmem((640, 1024), F32),
             vmem((640, 1024)),
             vmem((640, 1024)),
@@ -1088,26 +1203,31 @@
             vmem((2, 160, 1024), F32),
             vmem((2, 4, 256, 512)),
             vmem((2, 4, 512, 256)),
-            vmem((2, 2, 256, 512)),
-            vmem((2, 2, 512, 256)),
+            vmem((2, 2, 2, 256, 512)),
+            vmem((2, 2, 2, 512, 256)),
             vmem((2, 256, 512)),
             vmem((2, 512, 256)),
             vmem((2, 256, 512)),
             vmem((2, 512, 256)),
-            pltpu.SemaphoreType.DMA((96,)),
-            pltpu.SemaphoreType.DMA((96,)),
+            vmem((2, 256, 512)),
+            vmem((2, 512, 256)),
+            pltpu.SemaphoreType.DMA((208,)),
+            pltpu.SemaphoreType.DMA((208,)),
             pltpu.SemaphoreType.DMA((12,)),
         ],
         compiler_params=pltpu.CompilerParams(
             collective_id=0, has_side_effects=True, vmem_limit_bytes=VMEM_LIMIT
         ),
-    )(meta, tokens[0], cotangent[0], rts, wq, output_weight, expert_up[0], expert_down[0])
+    )(
+        sequence_lengths[0], block_order[0], tokens[0], cotangent[0], routes.reshape(1, 128),
+        project_weight, output_weight, ext, expert_up[0], expert_down[0],
+    )
     out_shapes = [
         ((128, 1024), BF),
         ((128, 1024), F32),
-        ((2, 32, 1536), F32),
+        ((32, 3072), F32),
         ((32, 1024), F32),
-        ((32, EXTRA), F32),
+        ((8, EXTRA), F32),
         ((2, 256, 1024), F32),
         ((2, 1024, 256), F32),
     ]
@@ -1128,10 +1248,6 @@
             vmem((256, 1024), F32),
             vmem((128, 1024)),
             vmem((128, 1024)),
-            vmem((2, 2, 256, 512)),
-            vmem((2, 2, 512, 256)),
-            vmem((2, 256, 512)),
-            vmem((2, 512, 256)),
             vmem((2, 256, 512)),
             vmem((2, 512, 256)),
             vmem((2, 256, 512)),
@@ -1152,6 +1268,7 @@
             vmem((128, 1024)),
             vmem((128, 1024)),
             vmem((3, 32, 1024)),
+            vmem((EXTRA, EXTRA), F32),
             pltpu.SemaphoreType.DMA((48,)),
             pltpu.SemaphoreType.DMA((48,)),
         ],
@@ -1159,14 +1276,13 @@
             collective_id=1, has_side_effects=True, vmem_limit_bytes=VMEM_LIMIT
         ),
     )(*mid)
-    project_grad = pgrad.reshape(2, 32, 3, 4, 128).transpose(1, 2, 3, 0, 4).reshape(32, 3072)
     return (
         out[None],
         tgrad[None],
-        egrad[:, 0],
-        project_grad,
+        egrad[0, :32],
+        pgrad,
         ograd,
-        egrad[:, 1:3].T,
+        egrad[1:3, :32],
         ugrad[None],
         dgrad[None],
     )

time: 379 us -> 295 us (0.78)
  Pallas kernels: 360 us -> 281 us
    pallas_call x1, Pallas kernels: 268 us -> 206 us  [fast_shards(): pl.pallas_call(forward_kernel, name='forward', out_shape=[shape(*s) for s...]
    pallas_call x1, Pallas kernels: 92.3 us -> 74.9 us  [fast_shards(): pl.pallas_call(backward_kernel, name='backward', out_shape=[shape(*s) for...]
    unnamed x14 -> x12, local copies, waits for them, and re-layouts: 7.43 us -> 9.65 us
where the time goes in v2:
time: 295 us
  Pallas kernels  281 us (95%)
  local copies, waits for them, and re-layouts  12.2 us (4%)
    pallas_call x1, Pallas kernels, fast_shards(): pl.pallas_call(forward_kernel, name='forward', out_shape=[shape(*s) for s...  206 us
    pallas_call x1, Pallas kernels, fast_shards(): pl.pallas_call(backward_kernel, name='backward', out_shape=[shape(*s) for...  74.9 us
    unnamed x12, local copies, waits for them, and re-layouts  9.65 us

profile of v2, /device:TPU:0, one launch (start us, length us, event | category | flops | bytes accessed | tf_op | source)
XLA Modules:
  0.0 295.0 jit_solution(7296930912909562814)
XLA Ops:
  0.6 1.3 fusion.6.ext
  1.9 206.0 %forward.1 = (bf16[256,1024]{1,0:T(8,128)(2,1)}, bf16[256,1536]{1,0:T(8,128)(2,1)}, f32[8,256,256]{2,1,0:T(8,128)}, bf16[2,256,512]{2,1,0:T(8,128)(2,1)}, bf16[1...) custom-call(s32[3]{0:T(128)} %bitcast.22, ...), custom_call_target="tpu_custom_call" | custom-call | tf_op jit(solution)/shard_map/forward/pallas_call | solution.py:1172
  207.9 74.9 %backward.1 = (bf16[128,1024]{1,0:T(8,128)(2,1)}, f32[128,1024]{1,0:T(8,128)}, f32[32,3072]{1,0:T(8,128)}, f32[32,1024]{1,0:T(8,128)}, f32[8,128]{1,0:T(8,128)},...) custom-call(bf16[256,1024]{1,0:T(8,128)(2,1)} %get-tuple-element.33.XG, bf16[256,1536]{1,0:T(8,128)(2,1)} %get-tuple-element.34.QKV, ...), custom_call_target="tpu_custom_call" | custom-call | tf_op jit(solution)/shard_map/backward/pallas_call | solution.py:1234
  282.8 0.0 copy-start.2
  282.8 0.0 copy-start.1
  282.8 1.3 slice_bitcast_fusion
  284.1 1.2 slice.7
  285.4 1.7 copy.25
  287.0 1.9 copy.26
  288.9 1.8 copy.27
  290.7 0.0 copy-done.2
  290.7 0.7 copy.28
  291.3 0.0 copy-done.1
  291.3 0.0 copy-start
  291.3 1.3 copy.29
  292.7 1.0 copy-done
  293.7 1.3 copy.30
Async XLA Ops:
  282.8 7.9 %copy-start.2 = (f32[32,1024]{1,0:T(8,128)S(1)}, f32[32,1024]{1,0:T(8,128)}, u32[]{:S(2)}) copy-start(f32[32,1024]{1,0:T(8,128)} %get-tuple-element.70) | copy-start | bytes 393220
  282.8 8.6 %copy-start.1 = (f32[2,256,1024]{2,1,0:T(8,128)S(1)}, f32[2,256,1024]{2,1,0:T(8,128)}, u32[]{:S(2)}) copy-start(f32[2,256,1024]{2,1,0:T(8,128)} %get-tuple-element.56) | copy-start | bytes 6291460
  291.3 2.3 copy-start

commit v3 on v2

--- a/solution.py
+++ b/solution.py
@@ -281,7 +281,8 @@
     )
 
 
-VMEM_LIMIT = 60 * 2**20
+VMEM_LIMIT = 61 * 2**20
+CHUNKS = (384, 384, 384, 512)
 
 IN_SPECS = (
     P(("grp", "wsh"), "ctx", None),
@@ -419,7 +420,9 @@
 
 def forward_kernel(
     lengths, order, tok, cot, rts, pw, wo_in, ext, up_in, dn_in,
-    XG, QKV, PR, MXH, W0, W1, W2, WO, RT, OUTS, RESS, CGR, P1U, P1D, Z1U, Z1D, S2U, S2D,
+    xg_out, qkv_out, pr_out, mxh_out, w0_out, w1_out, w2_out, wo_out,
+    RT, OUTS, RESS, CGR, P1U, P1D, Z1U, Z1D, S2U, S2D,
+    XG, QKV, PR, MXH, W0, W1, W2, WO,
     WS0, WS1, WS2, CG, XH, NRM, UP, DN, DSP, XS, GS, MS, AA,
     R1, R2, R3, R4, RB, PS, OWN, RES, GP1, A1, A2, DH, SUMS,
     GU, GD, CRU, CRD, P2U, P2D, ZSU, ZSD, ZRU, ZRD,
@@ -474,7 +477,6 @@
         )
 
     yw = [go(cp.new(WS[ch].at[1 - y], W[ch].at[row(y), :], p.dev_y)) for ch in range(3)]
-    zo = sum((go(cp.new(wo_in, WO.at[y, row_o, :], p.dev_z(k))) for k in (2, 1, 3)), ())
     zw = [z_rows(0, y), (), ()]
     ty = go(cp.new(RT.at[y], RT.at[y], p.dev_y), cp.new(tok, XG.at[mine, :], p.dev_y))
 
@@ -485,7 +487,7 @@
     other = pl.ds(pl.multiple_of((1 - x) * 512, 512), 512)
 
     def e_first(s):
-        return go(
+        return (
             cp.new(up_in.at[s, :, other], UP.at[s, 0, dq(g), :], p.dev_x),
             cp.new(dn_in.at[s, other, :], DN.at[s, 0, :, dq(g)], p.dev_x),
         )
@@ -503,7 +505,7 @@
         )
 
     def e_z(s):
-        return go(
+        return (
             cp.new(up_in.at[s, :, half], UP.at[s, 1, dq(g), :], p.dev_pair),
             cp.new(dn_in.at[s, half, :], DN.at[s, 1, :, dq(g)], p.dev_pair),
         )
@@ -520,13 +522,16 @@
             cp.new(DN.at[s, q, :, dq(which)], DN.at[s, q, :, dq(which)], p.dev_c),
         )
 
+    e1 = [e_first(0), e_first(1)]
+    go(*e1[0])
     wait(*yw[0])
     zw[0] += z_rows(0, 1 - y)
     for ch in (1, 2):
         wait(*yw[ch])
         zw[ch] = z_rows(ch, y) + z_rows(ch, 1 - y)
+    zo = sum((go(cp.new(wo_in, WO.at[y, row_o, :], p.dev_z(k))) for k in (2, 1, 3)), ())
     el = e_local(0) + e_local(1)
-    ec0 = [e_core0(0)]
+    ec0 = [e_core0(0), e_core0(1)]
 
     wait(*ty)
     values = XG[...].astype(F32)
@@ -547,20 +552,12 @@
         return cp.new(W[ch].at[dq(d), :], W[ch].at[dq(d), :], device)
 
     xw, fw = [None] * 3, [None] * 3
+    for ch in range(3):
+        wait(*zw[ch])
+        xw[ch] = go(w_copy(ch, g, p.dev_x), w_copy(ch, g, p.dev_c))
     wait(*zo)
-    xo = go(wo_copy(y, g, p.dev_x))
-    wait(*zw[0])
-    xw[0] = go(w_copy(0, g, p.dev_x), w_copy(0, g, p.dev_c))
-    wait(*xo)
-    yo = go(wo_copy(y, g, p.dev_y), wo_copy(y, p.gx, p.dev_y))
-    co = go(wo_copy(y, g, p.dev_c), wo_copy(y, p.gx, p.dev_c))
-    wait(*zw[1])
-    xw[1] = go(w_copy(1, g, p.dev_x), w_copy(1, g, p.dev_c))
-    wait(*zw[2])
-    xw[2] = go(w_copy(2, g, p.dev_x), w_copy(2, g, p.dev_c))
-    ez = [e_z(0), e_z(1)]
-    e1 = [e_first(0), e_first(1)]
-    ec0.append(e_core0(1))
+    yo = go(wo_copy(y, g, p.dev_y))
+    ez = [go(*e_z(0)), e_z(1)]
     cy = go(cp.new(cot, CG.at[mine, :], p.dev_y))
     wait(*xw[0])
     fw[0] = go(w_copy(0, p.gx, p.dev_c))
@@ -579,7 +576,15 @@
     wait(*fw[1])
     project(1)
     wait(*yo)
-    co += go(wo_copy(1 - y, g, p.dev_c), wo_copy(1 - y, p.gx, p.dev_c))
+    xo = go(
+        cp.new(WO.at[:, quarter(g), :], WO.at[:, quarter(g), :], p.dev_x),
+        cp.new(WO.at[:, quarter(g), :], WO.at[:, quarter(g), :], p.dev_c),
+    )
+    go(*e1[1])
+    wait(*e1[0])
+    er = [e_relay(0)]
+    ec = [e_core(0, 0, p.gx)]
+    go(*ez[1])
     wait(*xw[2])
     fw[2] = go(w_copy(2, p.gx, p.dev_c))
     wait(*fw[2])
@@ -619,19 +624,27 @@
         for b in (0, 1):
             MS[yy, b * CAP : (b + 1) * CAP, :] = dot(DSP[b], MXH[yy, b * 128 : (b + 1) * 128, :]).astype(BF)
 
-    wait(*e1[0])
-    er = [e_relay(0)]
-    ec = [e_core(0, 0, p.gx)]
     mixed_pick(y)
     wait(*cy)
     for b in (0, 1):
         GS[b * CAP : (b + 1) * CAP, :] = dot(DSP[b], CG[b * 128 : (b + 1) * 128, :]).astype(BF)
+    wait(*xo)
+    co = go(cp.new(WO.at[:, quarter(p.gx), :], WO.at[:, quarter(p.gx), :], p.dev_c))
     wait(*co)
     AA[...] = XS[...] + dot(MS[y], WO[y])
     lax.fori_loop(0, 4, lambda t, carry: (mixed_copy(t).wait(), carry)[1], 0)
     mixed_pick(1 - y)
     AA[...] += dot(MS[1 - y], WO[1 - y])
     gate = jax.nn.sigmoid(jnp.sum(AA[...] * centroid, axis=1, keepdims=True))
+
+    early = [
+        here(src, dst)
+        for src, dst in (
+            (XG, xg_out), (QKV, qkv_out), (PR, pr_out), (MXH, mxh_out),
+            (W0, w0_out), (W1, w1_out), (W2, w2_out), (WO, wo_out),
+        )
+    ]
+    go(*early)
 
     wait(*el)
     at_me, at_x, at_z, at_d = p.team_places()
@@ -741,15 +754,15 @@
 
     OWN[0] = first_forward(at_me)
     each(g1.relay_part)
+    wait(*e1[1])
+    er.append(e_relay(1))
+    ec.append(e_core(1, 0, p.gx))
     each(lambda i: g1.x(i).wait())
     PS[0, 0] = first_forward(at_x).astype(BF)
     OWN[3] = first_forward(at_z)
     each(lambda i: g1.forward(i).wait())
     PS[0, 1] = first_forward(at_d).astype(BF)
     r1.start_x()
-    wait(*e1[1])
-    er.append(e_relay(1))
-    ec.append(e_core(1, 0, p.gx))
     each(lambda i: r1.relay_part(i, OWN.at[3]))
     each(lambda i: g3.x(i).start())
     r1.x().wait()
@@ -914,25 +927,27 @@
     for k in (0, 1):
         S2U[k] = P2U[k].astype(F32) + ZRU[k].astype(F32)
         S2D[k] = P2D[k].astype(F32) + ZRD[k].astype(F32)
+    wait(*early)
 
 
 def backward_kernel(
-    XG, QKV, PR, MXH, W0, W1, W2, WO, RT, OUTS, RESS, CGR, P1U, P1D, Z1U, Z1D, S2U, S2D,
+    xg_in, qkv_in, pr_in, mxh_in, w0_in, w1_in, w2_in, wo_in,
+    RT, OUTS, RESS, CGR, P1U, P1D, Z1U, Z1D, S2U, S2D,
     out, tgrad, pgrad, ograd, egrad, ugrad, dgrad,
-    RP, OP, RL, XH, NRM, MG, DQ, NG, NGS, NGR,
+    XG, QKV, PR, MXH, W0, W1, W2, WO,
+    RP, OP, RL, XH, NRM, NRMT, MG, DQ, DT, NG, NGS, NGR,
     ZRU, ZRD, XSU, XSD, XRU, XRD,
-    PW, PC, PXS, PXR, PYS, PYR, PK, PZR,
+    PW0, PW1, PW2, PW3, PC0, PC1, PC2, PC3, PXS0, PXS1, PXS2, PXS3, PXR0, PXR1, PXR2, PXR3,
+    PYS0, PYS1, PYS2, PYS3, PK0, PK1, PK2, PK3, PZ0, PZ1, PZ2, PZ3,
     OW, OC, OXS, OXR, OK, OZR, TE,
-    send, recv,
+    send, recv, local,
 ):
+    PW, PC, PXS, PXR = (PW0, PW1, PW2, PW3), (PC0, PC1, PC2, PC3), (PXS0, PXS1, PXS2, PXS3), (PXR0, PXR1, PXR2, PXR3)
+    PYS, PK, PZ = (PYS0, PYS1, PYS2, PYS3), (PK0, PK1, PK2, PK3), (PZ0, PZ1, PZ2, PZ3)
     p = Place()
     g, y, w, x = p.g, p.y, p.w, p.x
     cp = Copies(send, recv)
-    W = (W0, W1, W2)
     all_in = greet([p.dev_x, p.dev_c, p.dev_y, p.dev_z(1), p.dev_z(2), p.dev_z(3)])
-    XSU[1] = S2U[1].astype(BF)
-    XSD[1] = S2D[1].astype(BF)
-    all_in()
 
     def go(*items):
         for item in items:
@@ -942,6 +957,20 @@
     def wait(*items):
         for item in items:
             item.wait()
+
+    loads = [
+        copy_in(src, dst, local.at[i])
+        for i, (src, dst) in enumerate(
+            (
+                (xg_in, XG), (w0_in, W0), (wo_in, WO), (mxh_in, MXH),
+                (qkv_in, QKV), (pr_in, PR), (w1_in, W1), (w2_in, W2),
+            )
+        )
+    ]
+    go(*loads)
+    XSU[1] = S2U[1].astype(BF)
+    XSD[1] = S2D[1].astype(BF)
+    all_in()
 
     own_slots = pl.ds(pl.multiple_of(y * CAP, 16), CAP)
     peer_slots = pl.ds(pl.multiple_of((1 - y) * CAP, 16), CAP)
@@ -958,9 +987,8 @@
 
     half = pl.ds(pl.multiple_of(x * 512, 512), 512)
     other = pl.ds(pl.multiple_of((1 - x) * 512, 512), 512)
-    ugrad[1, :, half] = S2U[0]
-    dgrad[1, half, :] = S2D[0]
-
+
+    wait(loads[0], loads[1])
     values = XG[...].astype(F32)
     centred = values - jnp.mean(values, axis=1, keepdims=True)
     inverse = lax.rsqrt(jnp.mean(centred * centred, axis=1, keepdims=True) + 1e-05)
@@ -968,6 +996,9 @@
     pick = one_hot(8, EXTRA)
     gain = dot(pick, W0[:, 512:], NT)[0:1, :]
     NRM[...] = (XH[...] * gain).astype(BF)
+    NRMT[...] = NRM[...].T
+    ugrad[1, :, half] = S2U[0]
+    dgrad[1, half, :] = S2D[0]
 
     wait(*ry)
     for b in (0, 1):
@@ -976,26 +1007,27 @@
             dot(dispatch_block(RT[b], y), RESS[slots, :], TN)
             + dot(dispatch_block(RT[b], 1 - y), RP[slots, :], TN)
         ).astype(BF)
+    wait(loads[2])
     MG[...] = dot(RL[...], WO[y], NT).astype(BF)
 
     def rows4(d):
         return pl.ds(pl.multiple_of(d * 128, 128), 128)
 
+    def dq(d):
+        return pl.ds(pl.multiple_of(d * 256, 256), 256)
+
+    def row32(v):
+        return pl.ds(pl.multiple_of(v * 32, 32), 32)
+
     def out_rows(d):
         OW[rows4(d), :] = dot(MXH[y, :, rows4(d)], RL[...], TN).astype(BF)
 
-    for d in (p.gc, p.gd, g, p.gx):
-        out_rows(d)
-    oc = []
-    for k, theirs in enumerate((p.gc, p.gd)):
-        oc += go(cp.new(OW.at[rows4(theirs), :], OC.at[k], p.dev_c))
-
     low_half = lax.broadcasted_iota(jnp.int32, (256, 128), 1) < 64
 
-    def heads(t, carry):
-        c0 = pl.ds(pl.multiple_of(t * 128, 128), 128)
-        c1 = pl.ds(pl.multiple_of(512 + t * 128, 128), 128)
-        c2 = pl.ds(pl.multiple_of(1024 + t * 128, 128), 128)
+    def heads(t):
+        c0 = slice(t * 128, (t + 1) * 128)
+        c1 = slice(512 + t * 128, 512 + (t + 1) * 128)
+        c2 = slice(1024 + t * 128, 1024 + (t + 1) * 128)
         q2, k2, v2, m2 = QKV[:, c0], QKV[:, c1], QKV[:, c2], MG[:, c0]
         parts = []
         for i in (0, 1):
@@ -1011,50 +1043,85 @@
                     dot(probs.astype(BF), m2, TN),
                 )
             )
-        DQ[:, c0] = jnp.where(low_half, parts[0][0], parts[1][0]).astype(BF)
-        DQ[:, c1] = jnp.where(low_half, parts[0][1], parts[1][1]).astype(BF)
-        DQ[:, c2] = jnp.where(low_half, parts[0][2], parts[1][2]).astype(BF)
-        return carry
-
-    lax.fori_loop(0, 4, heads, 0)
-
+        for s, c in enumerate((c0, c1, c2)):
+            grad = jnp.where(low_half, parts[0][s], parts[1][s]).astype(BF)
+            DQ[:, c] = grad
+            DT[t, :, s * 128 : (s + 1) * 128] = grad
+
+    pc, px, py, pz = [None] * 4, [None] * 4, [None] * 4, [None] * 4
+
+    def to_core(t):
+        PW[t][:, :384] = dot(NRMT[...], DT[t]).astype(BF)
+        pc[t] = sum(
+            (go(cp.new(PW[t].at[dq(d), :], PC[t].at[k], p.dev_c)) for k, d in enumerate((p.gc, p.gd))), ()
+        )
+
+    def to_x(t):
+        wait(*pc[t])
+        PXS[t][...] = (PW[t][dq(p.gx), :].astype(F32) + PC[t][1].astype(F32)).astype(BF)
+        px[t] = go(cp.new(PXS[t], PXR[t], p.dev_x))
+
+    def summed(t, plane):
+        rows = rows4(plane)
+        full = pl.ds(pl.multiple_of(g * 256 + plane * 128, 128), 128)
+        total = PW[t][full, :].astype(F32) + PC[t][0, rows, :].astype(F32) + PXR[t][rows, :].astype(F32)
+        return total.astype(BF)
+
+    def to_y(t):
+        wait(*px[t])
+        PYS[t][...] = summed(t, 1 - y)
+        py[t] = go(cp.new(PYS[t], PK[t].at[1], p.dev_y))
+        PK[t][0] = summed(t, y)
+
+    def to_z(t):
+        wait(*py[t])
+        pz[t] = sum(
+            (
+                go(cp.new(PK[t].at[:, row32(lax.rem(w + k, 4)), :], PZ[t].at[k - 1], p.dev_z(k)))
+                for k in (2, 1, 3)
+            ),
+            (),
+        )
+
+    wait(loads[4], loads[5])
+    heads(0)
+    to_core(0)
+    wait(loads[3])
+    out_rows(p.gc)
+    out_rows(p.gd)
+    oc = sum((go(cp.new(OW.at[rows4(d), :], OC.at[k], p.dev_c)) for k, d in enumerate((p.gc, p.gd))), ())
+    heads(1)
+    to_core(1)
+    to_x(0)
+    out_rows(g)
+    out_rows(p.gx)
+    heads(2)
+    to_core(2)
+    to_x(1)
+    wait(*oc)
+    OXS[...] = (OW[rows4(p.gx), :].astype(F32) + OC[1].astype(F32)).astype(BF)
+    heads(3)
+
+    wait(loads[6], loads[7])
     NG[...] = (
         dot(DQ[:, :512], W0[:, :512], NT) + dot(DQ[:, 512:1024], W1[...], NT) + dot(DQ[:, 1024:], W2[...], NT)
     )
-    NGS[...] = NG[pl.ds(pl.multiple_of((1 - y) * 128, 128), 128), :].astype(BF)
+    NGS[...] = NG[rows4(1 - y), :].astype(BF)
     ny = go(cp.new(NGS, NGR, p.dev_y))
     gain_row = jnp.sum(NG[...] * XH[...], axis=0, keepdims=True)
-
     line = lax.broadcasted_iota(jnp.int32, (8, 1024), 0)
     stack = jnp.where(line == 0, gain_row, jnp.where(line == 1 + y, CGR[0:1, :], 0.0)).astype(BF)
-
-    def dq(d):
-        return pl.ds(pl.multiple_of(d * 256, 256), 256)
-
-    def weight_rows(d):
-        PW[dq(d), :1536] = dot(NRM[:, dq(d)], DQ[...], TN).astype(BF)
-
-    def weight_loop(t, carry):
-        d, cc = lax.rem(t, 2), lax.div(t, 2)
-        weight_rows(2 * d + (p.c * cc + (1 - p.c) * (1 - cc)))
-        return carry
-
-    PW[:, 1536:] = dot(stack, pick, TN).astype(BF)
-    lax.fori_loop(0, 2, weight_loop, 0)
-    pc = []
-    for k, theirs in enumerate((p.gc, p.gd)):
-        pc += go(cp.new(PW.at[dq(theirs), :], PC.at[k], p.dev_c))
-    lax.fori_loop(2, 4, weight_loop, 0)
-
-    wait(*oc)
-    OXS[...] = (OW[rows4(p.gx), :].astype(F32) + OC[1].astype(F32)).astype(BF)
+    PW3[:, 384:] = dot(stack, pick, TN).astype(BF)
+    to_core(3)
+    to_x(2)
+    to_y(0)
+    to_x(3)
     ox = go(cp.new(OXS, OXR, p.dev_x))
-    wait(*pc)
-    PXS[...] = (PW[dq(p.gx), :].astype(F32) + PC[1].astype(F32)).astype(BF)
-    px = go(cp.new(PXS, PXR, p.dev_x))
+    to_y(1)
+    to_z(0)
 
     wait(*ny)
-    own_rows = pl.ds(pl.multiple_of(y * 128, 128), 128)
+    own_rows = rows4(y)
     normed = XH[own_rows, :]
     mine = XG[own_rows, :].astype(F32)
     mine = mine - jnp.mean(mine, axis=1, keepdims=True)
@@ -1065,73 +1132,69 @@
         - jnp.mean(scaled, axis=1, keepdims=True)
         - normed * jnp.mean(scaled * normed, axis=1, keepdims=True)
     )
+    to_y(2)
+    to_z(1)
+
+    wait(*f1)
+    XSU[0] = (P1U[1].astype(F32) + ZRU[1].astype(F32)).astype(BF)
+    XSD[0] = (P1D[1].astype(F32) + ZRD[1].astype(F32)).astype(BF)
+    f2[0] = go(cp.new(XSU.at[0], XRU.at[0], p.dev_x), cp.new(XSD.at[0], XRD.at[0], p.dev_x))
     wait(*oy)
     route_own = RT[y]
     out[...] = (
         dot(dispatch_block(route_own, y), OUTS[own_slots, :], TN)
         + dot(dispatch_block(route_own, 1 - y), OP[...], TN)
     ).astype(BF)
+    to_y(3)
+    to_z(2)
+    ugrad[0, :, half] = P1U[0].astype(F32) + ZRU[0].astype(F32)
+    dgrad[0, half, :] = P1D[0].astype(F32) + ZRD[0].astype(F32)
+    wait(*f2[1])
+    ugrad[1, :, other] = XRU[1].astype(F32)
+    dgrad[1, other, :] = XRD[1].astype(F32)
+    to_z(3)
 
     wait(*ox)
     OK[...] = (OW[rows4(g), :].astype(F32) + OC[0].astype(F32) + OXR[...].astype(F32)).astype(BF)
-
-    def row32(v):
-        return pl.ds(pl.multiple_of(v * 32, 32), 32)
-
-    oz = []
-    for k in (1, 3, 2):
-        oz += go(cp.new(OK.at[row32(lax.rem(w + k, 4)), :], OZR.at[k - 1], p.dev_z(k)))
-    wait(*px)
-
-    def summed(part):
-        rows = pl.ds(pl.multiple_of(part * 128, 128), 128)
-        full = pl.ds(pl.multiple_of(g * 256 + part * 128, 128), 128)
-        total = PW[full, :].astype(F32) + PC[0, rows, :].astype(F32) + PXR[rows, :].astype(F32)
-        return total.astype(BF)
-
-    PYS[...] = summed(1 - y)
-    py = go(cp.new(PYS, PYR, p.dev_y))
-    PK[...] = summed(y)
-    pz = []
-    for k in (1, 3, 2):
-        pz += go(cp.new(PK.at[row32(lax.rem(w + k, 4)), :], PZR.at[k - 1, 0], p.dev_z(k)))
-    wait(*py)
-    for k in (1, 3, 2):
-        pz += go(cp.new(PYR.at[row32(lax.rem(w + k, 4)), :], PZR.at[k - 1, 1], p.dev_z(k)))
-
-    wait(*f1)
-    ugrad[0, :, half] = P1U[0].astype(F32) + ZRU[0].astype(F32)
-    dgrad[0, half, :] = P1D[0].astype(F32) + ZRD[0].astype(F32)
-    XSU[0] = (P1U[1].astype(F32) + ZRU[1].astype(F32)).astype(BF)
-    XSD[0] = (P1D[1].astype(F32) + ZRD[1].astype(F32)).astype(BF)
-    f2[0] = go(cp.new(XSU.at[0], XRU.at[0], p.dev_x), cp.new(XSD.at[0], XRD.at[0], p.dev_x))
-    for s in (1, 0):
-        wait(*f2[s])
-        ugrad[s, :, other] = XRU[s].astype(F32)
-        dgrad[s, other, :] = XRD[s].astype(F32)
-
+    oz = sum(
+        (go(cp.new(OK.at[row32(lax.rem(w + k, 4)), :], OZR.at[k - 1], p.dev_z(k))) for k in (2, 1, 3)), ()
+    )
+    own32 = row32(w)
+    for t in range(4):
+        wait(*pz[t])
+        sums = [
+            PK[t][i, own32, :].astype(F32)
+            + PZ[t][0, i].astype(F32)
+            + PZ[t][1, i].astype(F32)
+            + PZ[t][2, i].astype(F32)
+            for i in (0, 1)
+        ]
+        for plane in (0, 1):
+            kept = jnp.where(y == plane, sums[0], sums[1])
+            for s in range(3):
+                first = s * 1024 + t * 256 + plane * 128
+                pgrad[:, first : first + 128] = kept[:, s * 128 : (s + 1) * 128]
+        if t == 3:
+            TE[0:32, :] = sums[0][:, 384:] + sums[1][:, 384:]
+    egrad[...] = TE[...].T[0:8, :]
+    wait(*f2[0])
+    ugrad[0, :, other] = XRU[0].astype(F32)
+    dgrad[0, other, :] = XRD[0].astype(F32)
     wait(*oz)
-    own32 = row32(w)
-    ograd[...] = (
-        OK[own32, :].astype(F32) + OZR[0].astype(F32) + OZR[1].astype(F32) + OZR[2].astype(F32)
-    )
-    wait(*pz)
-    sums = []
-    for i, kept in enumerate((PK, PYR)):
-        sums.append(
-            kept[own32, :].astype(F32)
-            + PZR[0, i].astype(F32)
-            + PZR[1, i].astype(F32)
-            + PZR[2, i].astype(F32)
-        )
-    for plane in (0, 1):
-        kept = jnp.where(y == plane, sums[0], sums[1])
-        for ch in range(3):
-            for t in range(4):
-                first = ch * 1024 + t * 256 + plane * 128
-                pgrad[:, first : first + 128] = kept[:, ch * 512 + t * 128 : ch * 512 + (t + 1) * 128]
-    TE[0:32, :] = sums[0][:, 1536:] + sums[1][:, 1536:]
-    egrad[...] = TE[...].T[0:8, :]
+    ograd[...] = OK[own32, :].astype(F32) + OZR[0].astype(F32) + OZR[1].astype(F32) + OZR[2].astype(F32)
+
+
+def finish_kernel(
+    out, tgrad, pgrad, ograd, egrad, ugrad, dgrad, out2, tgrad2, gain, pgrad2, ograd2, cent, ugrad2, dgrad2
+):
+    out2[0] = out[...]
+    tgrad2[0] = tgrad[...]
+    pgrad2[...] = pgrad[...]
+    ograd2[...] = ograd[...]
+    gain[...] = egrad[0:1, :32]
+    cent[...] = egrad[1:3, :32]
+    ugrad2[0] = ugrad[...]
+    dgrad2[0] = dgrad[...]
 
 
 def vmem(shape, dtype=BF):
@@ -1174,8 +1237,9 @@
         name="forward",
         out_shape=[shape(*s) for s in mid_shapes],
         in_specs=[in_smem] * 2 + [in_vmem] * 6 + [in_any] * 2,
-        out_specs=[in_vmem] * len(mid_shapes),
-        scratch_shapes=[
+        out_specs=[in_any] * 8 + [in_vmem] * (len(mid_shapes) - 8),
+        scratch_shapes=[vmem(*s) for s in mid_shapes[:8]]
+        + [
             vmem((2, 32, 512 + EXTRA)),
             vmem((2, 32, 512)),
             vmem((2, 32, 512)),
@@ -1213,7 +1277,7 @@
             vmem((2, 512, 256)),
             pltpu.SemaphoreType.DMA((208,)),
             pltpu.SemaphoreType.DMA((208,)),
-            pltpu.SemaphoreType.DMA((12,)),
+            pltpu.SemaphoreType.DMA((24,)),
         ],
         compiler_params=pltpu.CompilerParams(
             collective_id=0, has_side_effects=True, vmem_limit_bytes=VMEM_LIMIT
@@ -1235,16 +1299,19 @@
         backward_kernel,
         name="backward",
         out_shape=[shape(*s) for s in out_shapes],
-        in_specs=[in_vmem] * len(mid_shapes),
+        in_specs=[in_any] * 8 + [in_vmem] * (len(mid_shapes) - 8),
         out_specs=[in_vmem] * len(out_shapes),
-        scratch_shapes=[
+        scratch_shapes=[vmem(*s) for s in mid_shapes[:8]]
+        + [
             vmem((160, 1024)),
             vmem((CAP, 1024)),
             vmem((256, 1024)),
             vmem((256, 1024), F32),
             vmem((256, 1024)),
+            vmem((1024, 256)),
             vmem((256, 512)),
             vmem((256, 1536)),
+            vmem((4, 256, 384)),
             vmem((256, 1024), F32),
             vmem((128, 1024)),
             vmem((128, 1024)),
@@ -1254,14 +1321,15 @@
             vmem((2, 512, 256)),
             vmem((2, 256, 512)),
             vmem((2, 512, 256)),
-            vmem((1024, 1536 + EXTRA)),
-            vmem((2, 256, 1536 + EXTRA)),
-            vmem((256, 1536 + EXTRA)),
-            vmem((256, 1536 + EXTRA)),
-            vmem((128, 1536 + EXTRA)),
-            vmem((128, 1536 + EXTRA)),
-            vmem((128, 1536 + EXTRA)),
-            vmem((3, 2, 32, 1536 + EXTRA)),
+        ]
+        + [vmem((1024, c)) for c in CHUNKS]
+        + [vmem((2, 256, c)) for c in CHUNKS]
+        + [vmem((256, c)) for c in CHUNKS]
+        + [vmem((256, c)) for c in CHUNKS]
+        + [vmem((128, c)) for c in CHUNKS]
+        + [vmem((2, 128, c)) for c in CHUNKS]
+        + [vmem((3, 2, 32, c)) for c in CHUNKS]
+        + [
             vmem((512, 1024)),
             vmem((2, 128, 1024)),
             vmem((128, 1024)),
@@ -1269,23 +1337,32 @@
             vmem((128, 1024)),
             vmem((3, 32, 1024)),
             vmem((EXTRA, EXTRA), F32),
-            pltpu.SemaphoreType.DMA((48,)),
-            pltpu.SemaphoreType.DMA((48,)),
+            pltpu.SemaphoreType.DMA((64,)),
+            pltpu.SemaphoreType.DMA((64,)),
+            pltpu.SemaphoreType.DMA((8,)),
         ],
         compiler_params=pltpu.CompilerParams(
             collective_id=1, has_side_effects=True, vmem_limit_bytes=VMEM_LIMIT
         ),
     )(*mid)
-    return (
-        out[None],
-        tgrad[None],
-        egrad[0, :32],
-        pgrad,
-        ograd,
-        egrad[1:3, :32],
-        ugrad[None],
-        dgrad[None],
-    )
+    out, tgrad, gain, pgrad, ograd, cent, ugrad, dgrad = pl.pallas_call(
+        finish_kernel,
+        name="finish",
+        out_shape=[
+            shape((1, 128, 1024), BF),
+            shape((1, 128, 1024), F32),
+            shape((1, 32), F32),
+            shape((32, 3072), F32),
+            shape((32, 1024), F32),
+            shape((2, 32), F32),
+            shape((1, 2, 256, 1024), F32),
+            shape((1, 2, 1024, 256), F32),
+        ],
+        in_specs=[in_vmem] * 7,
+        out_specs=[in_vmem] * 8,
+        compiler_params=pltpu.CompilerParams(vmem_limit_bytes=VMEM_LIMIT),
+    )(out, tgrad, pgrad, ograd, egrad, ugrad, dgrad)
+    return out, tgrad, gain[0], pgrad, ograd, cent, ugrad, dgrad
 
 
 def solution(mesh):

time: 295 us -> 267 us (0.905)
  Pallas kernels: 281 us -> 265 us
  local copies, waits for them, and re-layouts: 12.2 us -> 0 us
    pallas_call x1, Pallas kernels: 74.9 us -> 59.9 us  [fast_shards(): pl.pallas_call(backward_kernel, name='backward', out_shape=[shape(*s) for...]
    unnamed x12 -> x0, local copies, waits for them, and re-layouts: 9.65 us -> none
    pallas_call x1, Pallas kernels: 206 us -> 200 us  [fast_shards(): pl.pallas_call(forward_kernel, name='forward', out_shape=[shape(*s) for s...]
    pallas_call x0 -> x1, Pallas kernels: none -> 5.13 us  [fast_shards(): pl.pallas_call(finish_kernel, name='finish', out_shape=[shape((1, 128, 10...]
where the time goes in v3:
time: 267 us; the launch traced here: 266 us
  Pallas kernels  265 us (99%)
    pallas_call x1, Pallas kernels, fast_shards(): pl.pallas_call(forward_kernel, name='forward', out_shape=[shape(*s) for s...  200 us
    pallas_call x1, Pallas kernels, fast_shards(): pl.pallas_call(backward_kernel, name='backward', out_shape=[shape(*s) for...  59.9 us

profile of v3, /device:TPU:0, one launch (start us, length us, event | category | flops | bytes accessed | tf_op | source)
XLA Modules:
  0.0 266.5 jit_solution(11280482260549540780)
XLA Ops:
  0.6 1.3 fusion.6.ext
  1.9 199.5 %forward.1 = (bf16[256,1024]{1,0:T(8,128)(2,1)}, bf16[256,1536]{1,0:T(8,128)(2,1)}, f32[8,256,256]{2,1,0:T(8,128)}, bf16[2,256,512]{2,1,0:T(8,128)(2,1)}, bf16[1...) custom-call(s32[3]{0:T(128)} %bitcast.13, ...), custom_call_target="tpu_custom_call" | custom-call | tf_op jit(solution)/shard_map/forward/pallas_call | solution.py:1235
  201.4 59.9 %backward.1 = (bf16[128,1024]{1,0:T(8,128)(2,1)}, f32[128,1024]{1,0:T(8,128)}, f32[32,3072]{1,0:T(8,128)}, f32[32,1024]{1,0:T(8,128)}, f32[8,128]{1,0:T(8,128)},...) custom-call(bf16[256,1024]{1,0:T(8,128)(2,1)} %get-tuple-element.41.xg_in, bf16[256,1536]{1,0:T(8,128)(2,1)} %get-tuple-element.42.qkv_in, ...), custom_call_target="tpu_custom_call" | custom-call | tf_op jit(solution)/shard_map/backward/pallas_call | solution.py:1298
  261.3 5.1 %finish.1 = (bf16[1,128,1024]{2,1,0:T(8,128)(2,1)}, f32[1,128,1024]{2,1,0:T(8,128)}, f32[1,32]{1,0:T(1,128)}, f32[32,3072]{1,0:T(8,128)}, f32[32,1024]{1,0:T(8,1...) custom-call(bf16[128,1024]{1,0:T(8,128)(2,1)} %get-tuple-element.59.out, ...), custom_call_target="tpu_custom_call" | custom-call | tf_op jit(solution)/shard_map/finish/pallas_call | solution.py:1348

commit v4 on v3

--- a/solution.py
+++ b/solution.py
@@ -728,6 +728,7 @@
     each(lambda i: g1.x(i).start())
     R3[mine_r, :] = (gate * GS[...].astype(F32)).astype(BF)
     each(lambda i: g3.z(i).start())
+    each(lambda i: g3.x(i).start())
 
     wait(*ec0[0])
     wait(*ec[0])
@@ -764,7 +765,6 @@
     PS[0, 1] = first_forward(at_d).astype(BF)
     r1.start_x()
     each(lambda i: r1.relay_part(i, OWN.at[3]))
-    each(lambda i: g3.x(i).start())
     r1.x().wait()
 
     def middle_part(i):
@@ -1099,7 +1099,12 @@
     to_core(2)
     to_x(1)
     wait(*oc)
-    OXS[...] = (OW[rows4(p.gx), :].astype(F32) + OC[1].astype(F32)).astype(BF)
+    for k, d in enumerate((g, p.gx)):
+        OK[k] = (OW[rows4(d), :].astype(F32) + OC[k].astype(F32)).astype(BF)
+    oz = sum(
+        (go(cp.new(OK.at[:, row32(lax.rem(w + k, 4)), :], OZR.at[k - 1], p.dev_z(k))) for k in (2, 1, 3)), ()
+    )
+    own32 = row32(w)
     heads(3)
 
     wait(loads[6], loads[7])
@@ -1116,9 +1121,21 @@
     to_x(2)
     to_y(0)
     to_x(3)
-    ox = go(cp.new(OXS, OXR, p.dev_x))
     to_y(1)
     to_z(0)
+
+    wait(*oz)
+
+    def out_sum(k):
+        return (
+            OK[k, own32, :].astype(F32)
+            + OZR[0, k].astype(F32)
+            + OZR[1, k].astype(F32)
+            + OZR[2, k].astype(F32)
+        )
+
+    OXS[...] = out_sum(1).astype(BF)
+    ox = go(cp.new(OXS, OXR, p.dev_x))
 
     wait(*ny)
     own_rows = rows4(y)
@@ -1154,12 +1171,6 @@
     dgrad[1, other, :] = XRD[1].astype(F32)
     to_z(3)
 
-    wait(*ox)
-    OK[...] = (OW[rows4(g), :].astype(F32) + OC[0].astype(F32) + OXR[...].astype(F32)).astype(BF)
-    oz = sum(
-        (go(cp.new(OK.at[row32(lax.rem(w + k, 4)), :], OZR.at[k - 1], p.dev_z(k))) for k in (2, 1, 3)), ()
-    )
-    own32 = row32(w)
     for t in range(4):
         wait(*pz[t])
         sums = [
@@ -1180,8 +1191,8 @@
     wait(*f2[0])
     ugrad[0, :, other] = XRU[0].astype(F32)
     dgrad[0, other, :] = XRD[0].astype(F32)
-    wait(*oz)
-    ograd[...] = OK[own32, :].astype(F32) + OZR[0].astype(F32) + OZR[1].astype(F32) + OZR[2].astype(F32)
+    wait(*ox)
+    ograd[...] = out_sum(0) + OXR[...].astype(F32)
 
 
 def finish_kernel(
@@ -1332,10 +1343,10 @@
         + [
             vmem((512, 1024)),
             vmem((2, 128, 1024)),
-            vmem((128, 1024)),
-            vmem((128, 1024)),
-            vmem((128, 1024)),
-            vmem((3, 32, 1024)),
+            vmem((32, 1024)),
+            vmem((32, 1024)),
+            vmem((2, 128, 1024)),
+            vmem((3, 2, 32, 1024)),
             vmem((EXTRA, EXTRA), F32),
             pltpu.SemaphoreType.DMA((64,)),
             pltpu.SemaphoreType.DMA((64,)),

time: 267 us -> 262 us (0.981)
  Pallas kernels: 265 us -> 260 us
    pallas_call x1, Pallas kernels: 59.9 us -> 55.7 us  [fast_shards(): pl.pallas_call(backward_kernel, name='backward', out_shape=[shape(*s) for...]
where the time goes in v4:
time: 262 us
  Pallas kernels  260 us (99%)
    pallas_call x1, Pallas kernels, fast_shards(): pl.pallas_call(forward_kernel, name='forward', out_shape=[shape(*s) for s...  199 us
    pallas_call x1, Pallas kernels, fast_shards(): pl.pallas_call(backward_kernel, name='backward', out_shape=[shape(*s) for...  55.7 us

profile of v4, /device:TPU:0, one launch (start us, length us, event | category | flops | bytes accessed | tf_op | source)
XLA Modules:
  0.0 262.0 jit_solution(6556980463210379790)
XLA Ops:
  0.6 1.3 fusion.6.ext
  1.9 199.3 %forward.1 = (bf16[256,1024]{1,0:T(8,128)(2,1)}, bf16[256,1536]{1,0:T(8,128)(2,1)}, f32[8,256,256]{2,1,0:T(8,128)}, bf16[2,256,512]{2,1,0:T(8,128)(2,1)}, bf16[1...) custom-call(s32[3]{0:T(128)} %bitcast.13, ...), custom_call_target="tpu_custom_call" | custom-call | tf_op jit(solution)/shard_map/forward/pallas_call | solution.py:1246
  201.2 55.7 %backward.1 = (bf16[128,1024]{1,0:T(8,128)(2,1)}, f32[128,1024]{1,0:T(8,128)}, f32[32,3072]{1,0:T(8,128)}, f32[32,1024]{1,0:T(8,128)}, f32[8,128]{1,0:T(8,128)},...) custom-call(bf16[256,1024]{1,0:T(8,128)(2,1)} %get-tuple-element.41.xg_in, bf16[256,1536]{1,0:T(8,128)(2,1)} %get-tuple-element.42.qkv_in, ...), custom_call_target="tpu_custom_call" | custom-call | tf_op jit(solution)/shard_map/backward/pallas_call | solution.py:1309
  256.9 5.1 %finish.1 = (bf16[1,128,1024]{2,1,0:T(8,128)(2,1)}, f32[1,128,1024]{2,1,0:T(8,128)}, f32[1,32]{1,0:T(1,128)}, f32[32,3072]{1,0:T(8,128)}, f32[32,1024]{1,0:T(8,1...) custom-call(bf16[128,1024]{1,0:T(8,128)(2,1)} %get-tuple-element.59.out, ...), custom_call_target="tpu_custom_call" | custom-call | tf_op jit(solution)/shard_map/finish/pallas_call | solution.py:1359

commit v5 on v4

--- a/solution.py
+++ b/solution.py
@@ -585,11 +585,6 @@
     er = [e_relay(0)]
     ec = [e_core(0, 0, p.gx)]
     go(*ez[1])
-    wait(*xw[2])
-    fw[2] = go(w_copy(2, p.gx, p.dev_c))
-    wait(*fw[2])
-    project(2)
-
     place_q, seq_q = place_of(lengths, order, lax.broadcasted_iota(jnp.int32, (256, 256), 0))
     place_k, seq_k = place_of(lengths, order, lax.broadcasted_iota(jnp.int32, (256, 256), 1))
     allowed = (seq_q == seq_k) & (place_k <= place_q)
@@ -600,25 +595,31 @@
         cols = pl.ds(pl.multiple_of(t * 128, 128), 128)
         return cp.at(mixed_first + t, MXH.at[y, :, cols], MXH.at[y, :, cols], p.dev_y)
 
-    def heads(t, carry):
-        cols = pl.ds(pl.multiple_of(t * 128, 128), 128)
-        q2 = QKV[:, cols]
+    def weigh(t, carry):
+        q2 = QKV[:, pl.ds(pl.multiple_of(t * 128, 128), 128)]
         k2 = QKV[:, pl.ds(pl.multiple_of(512 + t * 128, 128), 128)]
-        v2 = QKV[:, pl.ds(pl.multiple_of(1024 + t * 128, 128), 128)]
-        parts = []
         for i in (0, 1):
             keep = low_half if i == 0 else ~low_half
             scores = dot(jnp.where(keep, q2, jnp.zeros_like(q2)), k2, NT) * 0.125
             scores = jnp.where(allowed, scores, -1000000000.0)
             exponent = jnp.exp(scores - jnp.max(scores, axis=1, keepdims=True))
-            probs = exponent / jnp.sum(exponent, axis=1, keepdims=True)
-            PR[2 * t + i] = probs
-            parts.append(dot(probs.astype(BF), v2))
-        MXH[y, :, cols] = jnp.where(low_half, parts[0], parts[1]).astype(BF)
+            PR[2 * t + i] = exponent / jnp.sum(exponent, axis=1, keepdims=True)
+        return carry
+
+    def mix(t, carry):
+        v2 = QKV[:, pl.ds(pl.multiple_of(1024 + t * 128, 128), 128)]
+        low_part, high_part = (dot(PR[2 * t + i].astype(BF), v2) for i in (0, 1))
+        MXH[y, :, pl.ds(pl.multiple_of(t * 128, 128), 128)] = jnp.where(low_half, low_part, high_part).astype(BF)
         mixed_copy(t).start()
         return carry
 
-    lax.fori_loop(0, 4, heads, 0)
+    lax.fori_loop(0, 2, weigh, 0)
+    wait(*xw[2])
+    fw[2] = go(w_copy(2, p.gx, p.dev_c))
+    lax.fori_loop(2, 4, weigh, 0)
+    wait(*fw[2])
+    project(2)
+    lax.fori_loop(0, 4, mix, 0)
 
     def mixed_pick(yy):
         for b in (0, 1):
@@ -816,7 +817,7 @@
     PS[1, 0] = second_forward(at_x).astype(BF)
     OWN[4] = second_forward(at_z)
     each(lambda i: r3.relay_part(i, OWN.at[3]))
-    r2.start_x()
+    each(lambda i: r2.d(i).start())
 
     def weight_grads(A, R, RG, GU, GD):
         def one(q, d):
@@ -874,7 +875,6 @@
         )
 
     each(lambda i: r2.relay_part(i, OWN.at[4]))
-    r2.x().wait()
 
     def first_backward(place):
         at = rows_of(place)
@@ -888,6 +888,7 @@
 
     OWN[0] = first_backward(at_me)
     each(g4.relay_part)
+    r2.x().start()
     each(lambda i: g4.x(i).wait())
     PS[0, 0] = first_backward(at_x).astype(BF)
     OWN[3] = first_backward(at_z)
@@ -909,6 +910,7 @@
     CGR[...] = jnp.zeros_like(CGR)
 
     each(lambda i: r4.relay_part(i, OWN.at[3]))
+    r2.x().wait()
     each(output_part)
     body1 = weight_grads(A1, R1, R4, GU, GD)
     lax.fori_loop(0, 4, body1, 0)

time: 262 us -> 262 us (level)
  no operation moved by 1% of the time
where the time goes in v5:
time: 262 us; the launch traced here: 261 us
  Pallas kernels  260 us (99%)
    pallas_call x1, Pallas kernels, fast_shards(): pl.pallas_call(forward_kernel, name='forward', out_shape=[shape(*s) for s...  199 us
    pallas_call x1, Pallas kernels, fast_shards(): pl.pallas_call(backward_kernel, name='backward', out_shape=[shape(*s) for...  55.8 us

profile of v5, /device:TPU:0, one launch (start us, length us, event | category | flops | bytes accessed | tf_op | source)
XLA Modules:
  0.0 261.4 jit_solution(15656279812062614247)
XLA Ops:
  0.6 1.3 fusion.6.ext
  1.9 198.6 %forward.1 = (bf16[256,1024]{1,0:T(8,128)(2,1)}, bf16[256,1536]{1,0:T(8,128)(2,1)}, f32[8,256,256]{2,1,0:T(8,128)}, bf16[2,256,512]{2,1,0:T(8,128)(2,1)}, bf16[1...) custom-call(s32[3]{0:T(128)} %bitcast.13, ...), custom_call_target="tpu_custom_call" | custom-call | tf_op jit(solution)/shard_map/forward/pallas_call | solution.py:1248
  200.5 55.8 %backward.1 = (bf16[128,1024]{1,0:T(8,128)(2,1)}, f32[128,1024]{1,0:T(8,128)}, f32[32,3072]{1,0:T(8,128)}, f32[32,1024]{1,0:T(8,128)}, f32[8,128]{1,0:T(8,128)},...) custom-call(bf16[256,1024]{1,0:T(8,128)(2,1)} %get-tuple-element.41.xg_in, bf16[256,1536]{1,0:T(8,128)(2,1)} %get-tuple-element.42.qkv_in, ...), custom_call_target="tpu_custom_call" | custom-call | tf_op jit(solution)/shard_map/backward/pallas_call | solution.py:1311
  256.3 5.1 %finish.1 = (bf16[1,128,1024]{2,1,0:T(8,128)(2,1)}, f32[1,128,1024]{2,1,0:T(8,128)}, f32[1,32]{1,0:T(1,128)}, f32[32,3072]{1,0:T(8,128)}, f32[32,1024]{1,0:T(8,1...) custom-call(bf16[128,1024]{1,0:T(8,128)(2,1)} %get-tuple-element.59.out, ...), custom_call_target="tpu_custom_call" | custom-call | tf_op jit(solution)/shard_map/finish/pallas_call | solution.py:1361

commit v6 on v5

--- a/solution.py
+++ b/solution.py
@@ -558,6 +558,9 @@
     wait(*zo)
     yo = go(wo_copy(y, g, p.dev_y))
     ez = [go(*e_z(0)), e_z(1)]
+    wait(*e1[0])
+    er = [e_relay(0)]
+    ec = [e_core(0, 0, p.gx)]
     cy = go(cp.new(cot, CG.at[mine, :], p.dev_y))
     wait(*xw[0])
     fw[0] = go(w_copy(0, p.gx, p.dev_c))
@@ -581,9 +584,6 @@
         cp.new(WO.at[:, quarter(g), :], WO.at[:, quarter(g), :], p.dev_c),
     )
     go(*e1[1])
-    wait(*e1[0])
-    er = [e_relay(0)]
-    ec = [e_core(0, 0, p.gx)]
     go(*ez[1])
     place_q, seq_q = place_of(lengths, order, lax.broadcasted_iota(jnp.int32, (256, 256), 0))
     place_k, seq_k = place_of(lengths, order, lax.broadcasted_iota(jnp.int32, (256, 256), 1))

time: 262 us -> 262 us (level)
  no operation moved by 1% of the time
where the time goes in v6:
time: 262 us; the launch traced here: 261 us
  Pallas kernels  260 us (99%)
    pallas_call x1, Pallas kernels, fast_shards(): pl.pallas_call(forward_kernel, name='forward', out_shape=[shape(*s) for s...  199 us
    pallas_call x1, Pallas kernels, fast_shards(): pl.pallas_call(backward_kernel, name='backward', out_shape=[shape(*s) for...  55.8 us

profile of v6, /device:TPU:0, one launch (start us, length us, event | category | flops | bytes accessed | tf_op | source)
XLA Modules:
  0.0 261.4 jit_solution(17343909383106986790)
XLA Ops:
  0.6 1.3 fusion.6.ext
  1.9 198.6 %forward.1 = (bf16[256,1024]{1,0:T(8,128)(2,1)}, bf16[256,1536]{1,0:T(8,128)(2,1)}, f32[8,256,256]{2,1,0:T(8,128)}, bf16[2,256,512]{2,1,0:T(8,128)(2,1)}, bf16[1...) custom-call(s32[3]{0:T(128)} %bitcast.13, ...), custom_call_target="tpu_custom_call" | custom-call | tf_op jit(solution)/shard_map/forward/pallas_call | solution.py:1248
  200.5 55.8 %backward.1 = (bf16[128,1024]{1,0:T(8,128)(2,1)}, f32[128,1024]{1,0:T(8,128)}, f32[32,3072]{1,0:T(8,128)}, f32[32,1024]{1,0:T(8,128)}, f32[8,128]{1,0:T(8,128)},...) custom-call(bf16[256,1024]{1,0:T(8,128)(2,1)} %get-tuple-element.41.xg_in, bf16[256,1536]{1,0:T(8,128)(2,1)} %get-tuple-element.42.qkv_in, ...), custom_call_target="tpu_custom_call" | custom-call | tf_op jit(solution)/shard_map/backward/pallas_call | solution.py:1311
  256.3 5.1 %finish.1 = (bf16[1,128,1024]{2,1,0:T(8,128)(2,1)}, f32[1,128,1024]{2,1,0:T(8,128)}, f32[1,32]{1,0:T(1,128)}, f32[32,3072]{1,0:T(8,128)}, f32[32,1024]{1,0:T(8,1...) custom-call(bf16[128,1024]{1,0:T(8,128)(2,1)} %get-tuple-element.59.out, ...), custom_call_target="tpu_custom_call" | custom-call | tf_op jit(solution)/shard_map/finish/pallas_call | solution.py:1361
